TPU v7x, 256 devices: a whole 4x4x8 slice. The times are simulated.
256 devices in a mesh: dp: 16 (over y_lo, x, core), owner: 16 (over y_hi, z).
Axes of the slice: x: 4, y: 4 (y_hi: 2, y_lo: 2; y = y_hi * 2 + y_lo), z: 8, core: 2. Of those that a mesh axis runs over, the one named last changes fastest.
Arguments:
- acts: bfloat16 [16, 4096, 2560], P('owner', 'dp'), may hold values from -6 to 6
- outgrads: bfloat16 [16, 4096, 2560], P('owner', 'dp'), may hold values from -6 to 6
Outputs:
- update: bfloat16 [16, 2560, 2560], P(None, 'dp', 'owner')
All inputs are finite; a program needn't handle non-finite values.
Results may differ from a plain program's by a relative error of at most 0.0057.
Values may be sent and summed in bfloat16 or wider, within the bound.
No kernel may reach another device: no remote copies, remote signals or barrier semaphores. Data moves between devices by JAX's collectives and lax.ppermute only.
A program may use at most 128 MiB of HBM per device.

v0:
```python
import functools
import math

import jax
import jax.numpy as jnp
from jax import lax
from jax.experimental import pallas as pl
from jax.experimental.pallas import tpu as pltpu
from jax.sharding import PartitionSpec as P

BLK = 128
DAMPING = 0.1
TOKENS = 4096
D = 2560
HALF = D // 2
QUART = D // 4
NB = QUART // BLK
OUT = 160
PACK = 208
AXES = ("dp", "owner")
F32 = jnp.float32
BF16 = jnp.bfloat16
HI = lax.Precision.HIGHEST
VMEM = 60 * 2**20


def params():
    return pltpu.CompilerParams(vmem_limit_bytes=VMEM)


def pairs(move):
    result = []
    for d in range(16):
        for o in range(16):
            y, x, c, p = move(d // 8, (d // 2) % 4, d % 2, o)
            result.append((d * 16 + o, (y * 8 + x * 2 + c) * 16 + p))
    return result


def send(value, move):
    return lax.ppermute(value, AXES, pairs(move))


def swap_y(y, x, c, o):
    return 1 - y, x, c, o


def swap_core(y, x, c, o):
    return y, x, 1 - c, o


def swap_y_core(y, x, c, o):
    return 1 - y, x, 1 - c, o


def plus_x(y, x, c, o):
    return y, (x + 1) % 4, c, o


def minus_x(y, x, c, o):
    return y, (x + 3) % 4, c, o


def far_x(y, x, c, o):
    return y, (x + 2) % 4, c, o


def columns(value, index, width):
    return lax.dynamic_slice(value, (0, index * width), (value.shape[0], width))


def accumulate_kernel(plan, n_g, first, *refs):
    n = len(plan)
    a_refs, g_refs, refs = refs[:n], refs[n : n + n_g], refs[n + n_g :]
    if not first:
        prev_s, prev_m, refs = refs[0], refs[1], refs[2:]
    s_ref, m_ref = refs
    col = pl.ds(pl.multiple_of(pl.program_id(0) * BLK, BLK), BLK)
    s = jnp.zeros((BLK, QUART), F32) if first else prev_s[...]
    m_a = jnp.zeros((BLK, BLK), F32) if first else prev_m[0, 0]
    m_g = jnp.zeros((BLK, BLK), F32) if first else prev_m[0, 1]
    for a_ref, parts in zip(a_refs, plan):
        row = 0
        for which, start, size in parts:
            a = a_ref[row : row + size, :]
            g = g_refs[which][start : start + size, :]
            part = g_refs[which][start : start + size, col]
            at = a.T
            both = jnp.dot(at, jnp.concatenate([g, a], axis=1), preferred_element_type=F32)
            s += both[:, :QUART]
            m_a += both[:, QUART:]
            m_g += jnp.dot(part.T, part, preferred_element_type=F32)
            row += size
    s_ref[...] = s
    m_ref[0, 0] = m_a
    m_ref[0, 1] = m_g


def accumulate(a_list, plan, g_list, prev=None):
    s_spec = pl.BlockSpec((BLK, QUART), lambda i: (i, 0))
    m_spec = pl.BlockSpec((1, 2, BLK, BLK), lambda i: (i, 0, 0, 0))
    a_specs = [pl.BlockSpec((a.shape[0], BLK), lambda i: (0, i)) for a in a_list]
    g_specs = [pl.BlockSpec(g.shape, lambda i: (0, 0)) for g in g_list]
    extra = [] if prev is None else list(prev)
    tok = sum(a.shape[0] for a in a_list)
    return pl.pallas_call(
        functools.partial(accumulate_kernel, plan, len(g_list), prev is None),
        grid=(NB,),
        in_specs=a_specs + g_specs + ([s_spec, m_spec] if extra else []),
        out_specs=[s_spec, m_spec],
        out_shape=[
            jax.ShapeDtypeStruct((QUART, QUART), F32),
            jax.ShapeDtypeStruct((NB, 2, BLK, BLK), F32),
        ],
        compiler_params=params(),
        cost_estimate=pl.CostEstimate(
            flops=2 * tok * QUART * (QUART + 2 * BLK), bytes_accessed=tok * QUART * 4 + 8 * QUART * QUART, transcendentals=0
        ),
        name="accumulate",
    )(*a_list, *g_list, *extra)


def split(value):
    high = value.astype(BF16)
    return high, (value - high.astype(F32)).astype(BF16)


def dot_split(a, b):
    a_high, a_low = split(a)
    b_high, b_low = split(b)
    wide = jnp.concatenate([b_high, b_low], axis=1)
    both = jnp.dot(
        jnp.concatenate([a_high, a_low], axis=1),
        jnp.concatenate([wide, wide], axis=0),
        preferred_element_type=F32,
    )
    return both[:, :BLK] + both[:, BLK:]


def dot_left(a, b):
    a_high, a_low = split(a)
    b_high, b_low = split(b)
    total = jnp.dot(
        jnp.concatenate([a_high, a_low], axis=1),
        jnp.concatenate([b_high, b_high], axis=0),
        preferred_element_type=F32,
    )
    return total + jnp.dot(a_high, b_low, preferred_element_type=F32)


def finish_kernel(core, s_prev, m_prev, *refs):
    keep, give, inv, upd = refs[6:]
    tok = refs[2].shape[0]
    late = [(refs[n // 2], (n % 2) * tok, refs[2 + n]) for n in range(4)]
    rows = lax.broadcasted_iota(jnp.int32, (BLK, BLK), 0)
    cols = lax.broadcasted_iota(jnp.int32, (BLK, BLK), 1)
    eye = (rows == cols).astype(F32)
    errs, scales = [], []
    for i in range(NB):
        blk = slice(i * BLK, (i + 1) * BLK)
        total = s_prev[blk, :]
        m_a, m_g = m_prev[i, 0], m_prev[i, 1]
        for a_ref, row, g_ref in late:
            a, g = a_ref[row : row + tok, blk], g_ref[:, blk]
            at = a.T
            total += jnp.dot(at, g_ref[...], preferred_element_type=F32)
            m_a += jnp.dot(at, a, preferred_element_type=F32)
            m_g += jnp.dot(g.T, g, preferred_element_type=F32)
        upd[blk, :] = total
        for m in (m_a, m_g):
            m = m * (1.0 / TOKENS) + DAMPING * eye
            bound = jnp.max(jnp.sum(jnp.abs(m), axis=0, keepdims=True), axis=1, keepdims=True)
            scale = 1.0 / bound
            errs.append(eye - m * scale)
            scales.append(scale)
    prods = [eye + e for e in errs]
    errs = [dot_split(e, e) for e in errs]
    for step in range(3):
        if step < 2:
            both = [dot_split(jnp.concatenate([p, e], axis=0), e) for p, e in zip(prods, errs)]
            prods = [p + t[:BLK] for p, t in zip(prods, both)]
            errs = [t[BLK:] for t in both]
        else:
            prods = [p + dot_split(p, e) for p, e in zip(prods, errs)]
    for n in range(2 * NB):
        inv[n] = prods[n] * scales[n]
    for i in range(NB):
        blk = slice(i * BLK, (i + 1) * BLK)
        upd[blk, :] = dot_left(inv[2 * i].T, upd[blk, :])
    for j in range(NB):
        blk = slice(j * BLK, (j + 1) * BLK)
        upd[:, blk] = dot_split(upd[:, blk], inv[2 * j + 1]) * (1.0 / math.sqrt(TOKENS))
    for out, parity in ((keep, core[0]), (give, 1 - core[0])):
        for b in range(2):
            start = pl.multiple_of((2 * b + parity) * OUT, 32)
            strip = upd[pl.ds(start, OUT), :]
            for j in range(4):
                piece = strip[:, j * OUT : (j + 1) * OUT]
                tail = piece[:, BLK:]
                packed = jnp.concatenate([tail[q * 40 : (q + 1) * 40] for q in range(4)], axis=1)
                packed = jnp.concatenate([packed, jnp.zeros((8, BLK), F32)], axis=0)
                out[b, j, :OUT, :] = piece[:, :BLK].astype(BF16)
                out[b, j, OUT:, :] = packed.astype(BF16)


def finish(core, sums, a_late, g_arrays):
    tok = a_late[0].shape[0] // 2

    def whole(shape):
        return pl.BlockSpec(shape, lambda i, c: (0,) * len(shape))

    out = jax.ShapeDtypeStruct((2, 4, PACK, BLK), BF16)
    return pl.pallas_call(
        finish_kernel,
        grid_spec=pltpu.PrefetchScalarGridSpec(
            num_scalar_prefetch=1,
            grid=(1,),
            in_specs=[whole(v.shape) for v in (*sums, *a_late)] + [pl.BlockSpec((tok, QUART), lambda i, c: (3, 0))] * 4,
            out_specs=[whole(out.shape)] * 2,
            scratch_shapes=[pltpu.VMEM((2 * NB, BLK, BLK), F32), pltpu.VMEM((QUART, QUART), F32)],
        ),
        out_shape=[out] * 2,
        compiler_params=params(),
        cost_estimate=pl.CostEstimate(flops=2 * 10**9, bytes_accessed=5 * 10**6, transcendentals=0),
        name="finish",
    )(core, *sums, *a_late, *g_arrays)


def unpack_kernel(src, dst):
    for l in range(8):
        tail = src[l, OUT:, :].astype(F32)
        ext = jnp.concatenate([tail[:40, q * 32 : (q + 1) * 32] for q in range(4)], axis=0)
        dst[l, :, :BLK] = src[l, :OUT, :]
        dst[l, :, BLK:] = ext.astype(BF16)


def unpack(packed):
    return pl.pallas_call(
        unpack_kernel,
        grid=(2,),
        in_specs=[pl.BlockSpec((8, PACK, BLK), lambda i: (i, 0, 0))],
        out_specs=pl.BlockSpec((8, OUT, OUT), lambda i: (i, 0, 0)),
        out_shape=jax.ShapeDtypeStruct((16, OUT, OUT), BF16),
        compiler_params=params(),
        name="unpack",
    )(packed)


def after(value, *done):
    return lax.optimization_barrier((value, *done))[0]


def local(acts, outgrads):
    d = lax.axis_index("dp")
    y, x, c = d // 8, (d // 2) % 4, d % 2
    place = jnp.stack([c, x]).astype(jnp.int32)
    a_now, g_now = acts[0], outgrads[0]
    tok = a_now.shape[0]

    g_left = send(columns(g_now, (x + 1) % 4, QUART), plus_x)
    g_right = send(columns(g_now, (x + 3) % 4, QUART), minus_x)
    g_far = send(columns(g_now, (x + 2) % 4, QUART), far_x)
    mate = [
        send(columns(a_now, 2 * (1 - y) + c, QUART), swap_y),
        send(columns(a_now, 2 * (1 - y) + 1 - c, QUART), swap_y_core),
    ]
    own = [columns(a_now, 2 * y + c, QUART), send(columns(a_now, 2 * y + 1 - c, QUART), swap_core)]

    own_all = jnp.concatenate(own, axis=0)
    g_all = jnp.concatenate([columns(g_now, x, QUART), g_left, g_right, after(g_far, own_all)], axis=0)
    g_mate = send(after(g_all, *mate), swap_y)
    g_other = send(g_all, swap_core)

    mate_all = jnp.concatenate(mate, axis=0)
    own_left, own_right = send(own_all, plus_x), send(own_all, minus_x)
    mate_left, mate_right = send(mate_all, plus_x), send(mate_all, minus_x)
    own_far = send(own_left, plus_x)
    mate_far = send(mate_right, minus_x)
    g_mate_other = send(after(g_mate, own_left, own_right, mate_left, mate_right), swap_core)
    plan = [[(n, k * tok, tok), (n + 1, k * tok, tok)] for n in (0, 2) for k in range(3)]
    sums = accumulate(
        [own_all, own_left, own_right, mate_all, mate_left, mate_right], plan, [g_all, g_other, g_mate, g_mate_other]
    )
    keep, give = finish(place, sums, [own_far, mate_far], [g_all, g_other, g_mate, g_mate_other])
    recv = send(give, swap_core)
    got = []
    for k, move in enumerate([None, plus_x, far_x, minus_x]):
        target = (x + k) % 4
        strip = jnp.where(
            target // 2 == c,
            lax.dynamic_index_in_dim(keep, target % 2, 0, False),
            lax.dynamic_index_in_dim(recv, target % 2, 0, False),
        )
        got.append(strip if move is None else send(strip, move))
    pieces = jnp.zeros((16, PACK, BLK), BF16)
    for k in range(4):
        pieces = lax.dynamic_update_slice(pieces, got[k], (((x + 4 - k) % 4) * 4, 0, 0))
    return unpack(lax.all_to_all(pieces, "owner", split_axis=0, concat_axis=0, tiled=True))


def solution(mesh):
    return jax.shard_map(
        local,
        mesh=mesh,
        in_specs=(P("owner", "dp", None), P("owner", "dp", None)),
        out_specs=P(None, "dp", "owner"),
        check_vma=False,
    )
```

profile of v0, /device:TPU:38, one launch (start us, length us, event | category | flops | bytes accessed | tf_op | source)
XLA Modules:
  0.0 141.1 jit_solution(6296063449187280214)
XLA Ops:
  0.0 1.5 %dynamic-slice_bitcast_fusion.4 = (bf16[256,640]{1,0:T(8,128)(2,1)S(1)}, bf16[256,640]{1,0:T(8,128)(2,1)S(1)}, bf16[256,640]{1,0:T(8,128)(2,1)S(1)}, bf16[256,640]{1,0:T(8,128)(2,1)S(1)}) fusion(bf16[1,256,2560]{2,1,0:T(8,128)(2,1)} %param.2, s32[]{:T(128)S(6)} %select_n.187, s32[]{:T(128)S(6)} %select_n.185, s32[]{:T(128)S(6)} %select_n.184, s32[]{:T(128)S(6)} %select_n.186), kind=kLoop, calls=%fused_computation.6 | loop fusion | bytes 2621456 | tf_op jit(solution)/shard_map/dynamic_slice | solution.py:69
  1.5 0.1 collective-permute-start
  1.7 0.0 copy-done.4
  1.7 0.1 dynamic-slice_bitcast_fusion.3
  1.8 1.5 %collective-permute-start.9 = (bf16[256,640]{1,0:T(8,128)(2,1)S(1)}, bf16[256,640]{1,0:T(8,128)(2,1)S(1)}, u32[]{:S(2)}, u32[]{:S(2)}) collective-permute-start(bf16[256,640]{1,0:T(8,128)(2,1)S(1)} %get-tuple-element.21), channel_id=1, source_target_pairs={{0,64},{1,65},{2,66},{3,67},{4,68},{5,69},{6,70},{7,71},{8,72},{9,... | collective-permute-start | bytes 983048 | tf_op jit(solution)/shard_map/ppermute | solution.py:41
  3.3 2.1 %collective-permute-start.7 = (bf16[256,640]{1,0:T(8,128)(2,1)S(1)}, bf16[256,640]{1,0:T(8,128)(2,1)S(1)}, u32[]{:S(2)}, u32[]{:S(2)}) collective-permute-start(bf16[256,640]{1,0:T(8,128)(2,1)S(1)} %get-tuple-element.20), channel_id=1, source_target_pairs={{0,32},{1,33},{2,34},{3,35},{4,36},{5,37},{6,38},{7,39},{8,40},{9,... | collective-permute-start | bytes 983048 | tf_op jit(solution)/shard_map/ppermute | solution.py:41
  5.4 1.6 %collective-permute-start.3 = (bf16[256,640]{1,0:T(8,128)(2,1)S(1)}, bf16[256,640]{1,0:T(8,128)(2,1)S(1)}, u32[]{:S(2)}, u32[]{:S(2)}) collective-permute-start(bf16[256,640]{1,0:T(8,128)(2,1)S(1)} %get-tuple-element.26), channel_id=1, source_target_pairs={{0,128},{1,129},{2,130},{3,131},{4,132},{5,133},{6,134},{7,135},{8... | collective-permute-start | bytes 983048 | tf_op jit(solution)/shard_map/ppermute | solution.py:41
  7.0 0.1 pad_maximum_fusion.1.refs_0_
  7.1 6.9 %collective-permute-done.9 = bf16[256,640]{1,0:T(8,128)(2,1)S(1)} collective-permute-done((bf16[256,640]{1,0:T(8,128)(2,1)S(1)}, bf16[256,640]{1,0:T(8,128)(2,1)S(1)}, u32[]{:S(2)}, u32[]{:S(2)}) %collective-permute-start.9) | collective-permute-done | bytes 327712 | tf_op jit(solution)/shard_map/ppermute | solution.py:41
  14.0 4.3 %collective-permute-done.7 = bf16[256,640]{1,0:T(8,128)(2,1)S(1)} collective-permute-done((bf16[256,640]{1,0:T(8,128)(2,1)S(1)}, bf16[256,640]{1,0:T(8,128)(2,1)S(1)}, u32[]{:S(2)}, u32[]{:S(2)}) %collective-permute-start.7) | collective-permute-done | bytes 327712 | tf_op jit(solution)/shard_map/ppermute | solution.py:41
  18.3 2.2 %collective-permute-done.8 = bf16[256,640]{1,0:T(8,128)(2,1)S(1)} collective-permute-done((bf16[256,640]{1,0:T(8,128)(2,1)S(1)}, bf16[256,640]{1,0:T(8,128)(2,1)S(1)}, u32[]{:S(2)}, u32[]{:S(2)}) %collective-permute-start.8) | collective-permute-done | bytes 327712 | tf_op jit(solution)/shard_map/ppermute | solution.py:41
  20.4 0.1 pad_maximum_fusion.refs_6_.refs_2_
  20.6 0.0 copy-start
  20.6 0.0 collective-permute-done.3
  20.6 0.4 collective-permute-done.4
  21.0 1.3 collective-permute-start.11
  22.4 2.7 %collective-permute-start.5 = (bf16[512,640]{1,0:T(8,128)(2,1)S(1)}, bf16[512,640]{1,0:T(8,128)(2,1)S(1)}, u32[]{:S(2)}, u32[]{:S(2)}) collective-permute-start(bf16[512,640]{1,0:T(8,128)(2,1)S(1)} %constant_dynamic-update-slice_fusion.refs_3_), channel_id=1, source_target_pairs={{0,32},{1,33},{2,34},{3,35},{4,36},{5,37},{6,38},{7,39},{8,40},{9,... | collective-permute-start | bytes 1966088 | tf_op jit(solution)/shard_map/ppermute | solution.py:41
  25.1 0.0 collective-permute-start.6
  25.1 3.2 %collective-permute-start.1 = (bf16[512,640]{1,0:T(8,128)(2,1)S(1)}, bf16[512,640]{1,0:T(8,128)(2,1)}, u32[]{:S(2)}, u32[]{:S(2)}) collective-permute-start(bf16[512,640]{1,0:T(8,128)(2,1)S(1)} %pad_maximum_fusion.1.refs_0_), channel_id=1, source_target_pairs={{0,32},{1,33},{2,34},{3,35},{4,36},{5,37},{6,38},{7,39},{8,40},{9,... | collective-permute-start | bytes 1966088 | tf_op jit(solution)/shard_map/ppermute | solution.py:41
  28.3 0.0 collective-permute-start.2
  28.3 11.8 %collective-permute-done.5.refs_4_ = bf16[512,640]{1,0:T(8,128)(2,1)S(1)} collective-permute-done((bf16[512,640]{1,0:T(8,128)(2,1)S(1)}, bf16[512,640]{1,0:T(8,128)(2,1)S(1)}, u32[]{:S(2)}, u32[]{:S(2)}) %collective-permute-start.5) | collective-permute-done | bytes 655392 | tf_op jit(solution)/shard_map/ppermute | solution.py:41
  40.1 0.3 collective-permute-start.10
  40.4 3.6 %collective-permute-done.6.refs_5_ = bf16[512,640]{1,0:T(8,128)(2,1)} collective-permute-done((bf16[512,640]{1,0:T(8,128)(2,1)S(1)}, bf16[512,640]{1,0:T(8,128)(2,1)}, u32[]{:S(2)}, u32[]{:S(2)}) %collective-permute-start.6) | collective-permute-done | bytes 655392 | tf_op jit(solution)/shard_map/ppermute | solution.py:41
  44.0 10.2 %collective-permute-done.1.refs_1_ = bf16[512,640]{1,0:T(8,128)(2,1)} collective-permute-done((bf16[512,640]{1,0:T(8,128)(2,1)S(1)}, bf16[512,640]{1,0:T(8,128)(2,1)}, u32[]{:S(2)}, u32[]{:S(2)}) %collective-permute-start.1) | collective-permute-done | bytes 655392 | tf_op jit(solution)/shard_map/ppermute | solution.py:41
  54.2 3.6 %collective-permute-done.2.refs_2_ = bf16[512,640]{1,0:T(8,128)(2,1)S(1)} collective-permute-done((bf16[512,640]{1,0:T(8,128)(2,1)S(1)}, bf16[512,640]{1,0:T(8,128)(2,1)S(1)}, u32[]{:S(2)}, u32[]{:S(2)}) %collective-permute-start.2) | collective-permute-done | bytes 655392 | tf_op jit(solution)/shard_map/ppermute | solution.py:41
  57.7 0.0 collective-permute-done.11.refs_8_.refs_4_
  57.7 0.1 collective-permute-start.12
  57.8 0.1 collective-permute-start.14
  57.9 3.2 %collective-permute-start.13 = (bf16[512,640]{1,0:T(8,128)(2,1)}, bf16[512,640]{1,0:T(8,128)(2,1)}, u32[]{:S(2)}, u32[]{:S(2)}) collective-permute-start(bf16[512,640]{1,0:T(8,128)(2,1)} %collective-permute-done.1.refs_1_), channel_id=1, source_target_pairs={{0,32},{1,33},{2,34},{3,35},{4,36},{5,37},{6,38},{7,39},{8,40},{9,... | collective-permute-start | bytes 1966088 | tf_op jit(solution)/shard_map/ppermute | solution.py:41
  61.2 0.6 pad_add_fusion.core
  61.8 0.0 collective-permute-done.12.refs_9_.refs_5_
  61.9 1.0 copy-done.3
  62.9 9.7 %accumulate.1 = (f32[640,640]{1,0:T(8,128)}, f32[5,2,128,128]{3,2,1,0:T(8,128)}) custom-call(bf16[512,640]{1,0:T(8,128)(2,1)} %copy-done.5, bf16[512,640]{1,0:T(8,128)(2,1)} %collective-permute-done.1.refs_1_, bf16[512,640]{1,0:T(8,128)(2,1)} %copy-done.8, bf16[512,640]{1,0:T(8,128)(2,1)} %copy-done.6, bf16[512,640]{1,0:T(8,128)(2,1)} %copy-done.7, ...), custom_call_target="tpu_custom_call" | custom-call | flops 3523215360 | bytes 11141120 | tf_op jit(solution)/shard_map/accumulate/pallas_call | solution.py:106
  72.6 4.0 %collective-permute-done.14.refs_1_ = bf16[512,640]{1,0:T(8,128)(2,1)} collective-permute-done((bf16[512,640]{1,0:T(8,128)(2,1)}, bf16[512,640]{1,0:T(8,128)(2,1)}, u32[]{:S(2)}, u32[]{:S(2)}) %collective-permute-start.14) | collective-permute-done | bytes 655392 | tf_op jit(solution)/shard_map/ppermute | solution.py:41
  76.5 0.0 collective-permute-done.13.refs_0_
  76.5 8.5 %finish.1 = (bf16[2,4,208,128]{3,2,1,0:T(8,128)(2,1)}, bf16[2,4,208,128]{3,2,1,0:T(8,128)(2,1)}) custom-call(s32[2]{0:T(128)} %pad_add_fusion.core, f32[640,640]{1,0:T(8,128)} %get-tuple-element.15.s_prev, f32[5,2,128,128]{3,2,1,0:T(8,128)} %get-tuple-element.16.m_prev, bf16[512,640]{1,0:T(8,128)(2,1)} %collective-permute-done.13.refs_0_, ...), custom_call_target="tpu_custom_call" | custom-call | flops 2000000000 | bytes 5000000 | tf_op jit(solution)/shard_map/finish/pallas_call | solution.py:213
  85.0 0.0 collective-permute-start.15
  85.0 2.0 %collective-permute-done.15 = bf16[2,4,208,128]{3,2,1,0:T(8,128)(2,1)S(1)} collective-permute-done((bf16[2,4,208,128]{3,2,1,0:T(8,128)(2,1)}, bf16[2,4,208,128]{3,2,1,0:T(8,128)(2,1)S(1)}, u32[]{:S(2)}, u32[]{:S(2)}) %collective-permute-start.15) | collective-permute-done | bytes 426016 | tf_op jit(solution)/shard_map/ppermute | solution.py:41
  87.0 1.3 select_bitcast_fusion
  88.2 3.0 %collective-permute-start.16 = (bf16[4,208,128]{2,1,0:T(8,128)(2,1)S(1)}, bf16[4,208,128]{2,1,0:T(8,128)(2,1)S(1)}, u32[]{:S(2)}, u32[]{:S(2)}) collective-permute-start(bf16[4,208,128]{2,1,0:T(8,128)(2,1)S(1)} %get-tuple-element.29), channel_id=1, source_target_pairs={{0,32},{1,33},{2,34},{3,35},{4,36},{5,37},{6,38},{7,39},{8,40},{9,... | collective-permute-start | bytes 638984 | tf_op jit(solution)/shard_map/ppermute | solution.py:41
  91.3 1.0 collective-permute-start.18
  92.3 0.1 broadcast_in_dim.3
  92.4 0.1 bitcast_dynamic-update-slice_fusion
  92.5 8.1 %collective-permute-done.16 = bf16[4,208,128]{2,1,0:T(8,128)(2,1)S(1)} collective-permute-done((bf16[4,208,128]{2,1,0:T(8,128)(2,1)S(1)}, bf16[4,208,128]{2,1,0:T(8,128)(2,1)S(1)}, u32[]{:S(2)}, u32[]{:S(2)}) %collective-permute-start.16) | collective-permute-done | bytes 213024 | tf_op jit(solution)/shard_map/ppermute | solution.py:41
  100.7 0.2 collective-permute-done.17
  100.9 3.1 %collective-permute-done.18 = bf16[4,208,128]{2,1,0:T(8,128)(2,1)S(1)} collective-permute-done((bf16[4,208,128]{2,1,0:T(8,128)(2,1)S(1)}, bf16[4,208,128]{2,1,0:T(8,128)(2,1)S(1)}, u32[]{:S(2)}, u32[]{:S(2)}) %collective-permute-start.18) | collective-permute-done | bytes 213024 | tf_op jit(solution)/shard_map/ppermute | solution.py:41
  104.1 34.8 %all_to_all.5.src = bf16[16,208,128]{2,1,0:T(8,128)(2,1)} all-to-all(bf16[16,208,128]{2,1,0:T(8,128)(2,1)S(1)} %constant_dynamic-update-slice_fusion.4), channel_id=1, replica_groups=mesh['dp'=16,'owner'=16] {'owner'}, dimensions={0} | all-to-all | bytes 1703936 | tf_op jit(solution)/shard_map/all_to_all | solution.py:298
  138.9 2.2 %unpack.1 = bf16[16,160,160]{2,1,0:T(8,128)(2,1)} custom-call(bf16[16,208,128]{2,1,0:T(8,128)(2,1)} %all_to_all.5.src), custom_call_target="tpu_custom_call" | custom-call | tf_op jit(solution)/shard_map/unpack/pallas_call | solution.py:238
  (25 shorter events, 0.2 us)
Async XLA Ops:
  0.0 1.7 %copy-start.4 = (bf16[1,256,2560]{2,1,0:T(8,128)(2,1)S(1)}, bf16[1,256,2560]{2,1,0:T(8,128)(2,1)}, u32[]{:S(2)}) copy-start(bf16[1,256,2560]{2,1,0:T(8,128)(2,1)} %param.3) | copy-start | bytes 3932164
  1.5 5.5 %collective-permute-start = (bf16[256,640]{1,0:T(8,128)(2,1)S(1)}, bf16[256,640]{1,0:T(8,128)(2,1)S(1)}, u32[]{:S(2)}, u32[]{:S(2)}) collective-permute-start(bf16[256,640]{1,0:T(8,128)(2,1)S(1)} %get-tuple-element.24), channel_id=1, source_target_pairs={{0,16},{1,17},{2,18},{3,19},{4,20},{5,21},{6,22},{7,23},{8,24},{9,... | collective-permute-start | bytes 983048 | tf_op jit(solution)/shard_map/ppermute | solution.py:41
  1.8 12.2 %collective-permute-start.9 = (bf16[256,640]{1,0:T(8,128)(2,1)S(1)}, bf16[256,640]{1,0:T(8,128)(2,1)S(1)}, u32[]{:S(2)}, u32[]{:S(2)}) collective-permute-start(bf16[256,640]{1,0:T(8,128)(2,1)S(1)} %get-tuple-element.21), channel_id=1, source_target_pairs={{0,64},{1,65},{2,66},{3,67},{4,68},{5,69},{6,70},{7,71},{8,72},{9,... | collective-permute-start | bytes 983048 | tf_op jit(solution)/shard_map/ppermute | solution.py:41
  3.3 14.9 %collective-permute-start.7 = (bf16[256,640]{1,0:T(8,128)(2,1)S(1)}, bf16[256,640]{1,0:T(8,128)(2,1)S(1)}, u32[]{:S(2)}, u32[]{:S(2)}) collective-permute-start(bf16[256,640]{1,0:T(8,128)(2,1)S(1)} %get-tuple-element.20), channel_id=1, source_target_pairs={{0,32},{1,33},{2,34},{3,35},{4,36},{5,37},{6,38},{7,39},{8,40},{9,... | collective-permute-start | bytes 983048 | tf_op jit(solution)/shard_map/ppermute | solution.py:41
  5.4 15.0 %collective-permute-start.8 = (bf16[256,640]{1,0:T(8,128)(2,1)S(1)}, bf16[256,640]{1,0:T(8,128)(2,1)S(1)}, u32[]{:S(2)}, u32[]{:S(2)}) collective-permute-start(bf16[256,640]{1,0:T(8,128)(2,1)S(1)} %get-tuple-element.22), channel_id=1, source_target_pairs={{0,96},{1,97},{2,98},{3,99},{4,100},{5,101},{6,102},{7,103},{8,104... | collective-permute-start | bytes 983048 | tf_op jit(solution)/shard_map/ppermute | solution.py:41
  5.4 15.1 %collective-permute-start.3 = (bf16[256,640]{1,0:T(8,128)(2,1)S(1)}, bf16[256,640]{1,0:T(8,128)(2,1)S(1)}, u32[]{:S(2)}, u32[]{:S(2)}) collective-permute-start(bf16[256,640]{1,0:T(8,128)(2,1)S(1)} %get-tuple-element.26), channel_id=1, source_target_pairs={{0,128},{1,129},{2,130},{3,131},{4,132},{5,133},{6,134},{7,135},{8... | collective-permute-start | bytes 983048 | tf_op jit(solution)/shard_map/ppermute | solution.py:41
  7.0 14.0 %collective-permute-start.4 = (bf16[256,640]{1,0:T(8,128)(2,1)S(1)}, bf16[256,640]{1,0:T(8,128)(2,1)S(1)}, u32[]{:S(2)}, u32[]{:S(2)}) collective-permute-start(bf16[256,640]{1,0:T(8,128)(2,1)S(1)} %get-tuple-element.23), channel_id=1, source_target_pairs={{0,144},{1,145},{2,146},{3,147},{4,148},{5,149},{6,150},{7,151},{8... | collective-permute-start | bytes 983048 | tf_op jit(solution)/shard_map/ppermute | solution.py:41
  7.1 21.2 %copy-start.5 = (bf16[512,640]{1,0:T(8,128)(2,1)}, bf16[512,640]{1,0:T(8,128)(2,1)S(1)}, u32[]{:S(2)}) copy-start(bf16[512,640]{1,0:T(8,128)(2,1)S(1)} %pad_maximum_fusion.1.refs_0_) | copy-start | bytes 1966084
  20.6 41.3 %copy-start = (bf16[1024,640]{1,0:T(8,128)(2,1)}, bf16[1024,640]{1,0:T(8,128)(2,1)S(1)}, u32[]{:S(2)}) copy-start(bf16[1024,640]{1,0:T(8,128)(2,1)S(1)} %pad_maximum_fusion.refs_6_.refs_2_) | copy-start | bytes 3932164
  21.0 36.8 %collective-permute-start.11 = (bf16[1024,640]{1,0:T(8,128)(2,1)S(1)}, bf16[1024,640]{1,0:T(8,128)(2,1)S(1)}, u32[]{:S(2)}, u32[]{:S(2)}) collective-permute-start(bf16[1024,640]{1,0:T(8,128)(2,1)S(1)} %pad_maximum_fusion.refs_6_.refs_2_), channel_id=1, source_target_pairs={{0,128},{1,129},{2,130},{3,131},{4,132},{5,133},{6,134},{7,135},{8... | collective-permute-start | bytes 3932168 | tf_op jit(solution)/shard_map/ppermute | solution.py:41
  22.4 39.5 %copy-start.6 = (bf16[512,640]{1,0:T(8,128)(2,1)}, bf16[512,640]{1,0:T(8,128)(2,1)S(1)}, u32[]{:S(2)}) copy-start(bf16[512,640]{1,0:T(8,128)(2,1)S(1)} %constant_dynamic-update-slice_fusion.refs_3_) | copy-start | bytes 1966084
  22.4 17.7 %collective-permute-start.5 = (bf16[512,640]{1,0:T(8,128)(2,1)S(1)}, bf16[512,640]{1,0:T(8,128)(2,1)S(1)}, u32[]{:S(2)}, u32[]{:S(2)}) collective-permute-start(bf16[512,640]{1,0:T(8,128)(2,1)S(1)} %constant_dynamic-update-slice_fusion.refs_3_), channel_id=1, source_target_pairs={{0,32},{1,33},{2,34},{3,35},{4,36},{5,37},{6,38},{7,39},{8,40},{9,... | collective-permute-start | bytes 1966088 | tf_op jit(solution)/shard_map/ppermute | solution.py:41
  25.1 18.9 %collective-permute-start.6 = (bf16[512,640]{1,0:T(8,128)(2,1)S(1)}, bf16[512,640]{1,0:T(8,128)(2,1)}, u32[]{:S(2)}, u32[]{:S(2)}) collective-permute-start(bf16[512,640]{1,0:T(8,128)(2,1)S(1)} %constant_dynamic-update-slice_fusion.refs_3_), channel_id=1, source_target_pairs={{0,96},{1,97},{2,98},{3,99},{4,100},{5,101},{6,102},{7,103},{8,104... | collective-permute-start | bytes 1966088 | tf_op jit(solution)/shard_map/ppermute | solution.py:41
  25.1 29.1 %collective-permute-start.1 = (bf16[512,640]{1,0:T(8,128)(2,1)S(1)}, bf16[512,640]{1,0:T(8,128)(2,1)}, u32[]{:S(2)}, u32[]{:S(2)}) collective-permute-start(bf16[512,640]{1,0:T(8,128)(2,1)S(1)} %pad_maximum_fusion.1.refs_0_), channel_id=1, source_target_pairs={{0,32},{1,33},{2,34},{3,35},{4,36},{5,37},{6,38},{7,39},{8,40},{9,... | collective-permute-start | bytes 1966088 | tf_op jit(solution)/shard_map/ppermute | solution.py:41
  28.3 29.4 %collective-permute-start.2 = (bf16[512,640]{1,0:T(8,128)(2,1)S(1)}, bf16[512,640]{1,0:T(8,128)(2,1)S(1)}, u32[]{:S(2)}, u32[]{:S(2)}) collective-permute-start(bf16[512,640]{1,0:T(8,128)(2,1)S(1)} %pad_maximum_fusion.1.refs_0_), channel_id=1, source_target_pairs={{0,96},{1,97},{2,98},{3,99},{4,100},{5,101},{6,102},{7,103},{8,104... | collective-permute-start | bytes 1966088 | tf_op jit(solution)/shard_map/ppermute | solution.py:41
  40.1 21.7 %copy-start.7 = (bf16[512,640]{1,0:T(8,128)(2,1)}, bf16[512,640]{1,0:T(8,128)(2,1)S(1)}, u32[]{:S(2)}) copy-start(bf16[512,640]{1,0:T(8,128)(2,1)S(1)} %collective-permute-done.5.refs_4_) | copy-start | bytes 1966084
  40.1 21.7 %collective-permute-start.10 = (bf16[1024,640]{1,0:T(8,128)(2,1)S(1)}, bf16[1024,640]{1,0:T(8,128)(2,1)S(1)}, u32[]{:S(2)}, u32[]{:S(2)}) collective-permute-start(bf16[1024,640]{1,0:T(8,128)(2,1)S(1)} %pad_maximum_fusion.refs_6_.refs_2_), channel_id=1, source_target_pairs={{0,16},{1,17},{2,18},{3,19},{4,20},{5,21},{6,22},{7,23},{8,24},{9,... | collective-permute-start | bytes 3932168 | tf_op jit(solution)/shard_map/ppermute | solution.py:41
  57.7 4.1 %copy-start.8 = (bf16[512,640]{1,0:T(8,128)(2,1)}, bf16[512,640]{1,0:T(8,128)(2,1)S(1)}, u32[]{:S(2)}) copy-start(bf16[512,640]{1,0:T(8,128)(2,1)S(1)} %collective-permute-done.2.refs_2_) | copy-start | bytes 1966084
  57.7 4.1 %copy-start.2 = (bf16[1024,640]{1,0:T(8,128)(2,1)}, bf16[1024,640]{1,0:T(8,128)(2,1)S(1)}, u32[]{:S(2)}) copy-start(bf16[1024,640]{1,0:T(8,128)(2,1)S(1)} %collective-permute-done.11.refs_8_.refs_4_) | copy-start | bytes 3932164
  57.7 4.1 %collective-permute-start.12 = (bf16[1024,640]{1,0:T(8,128)(2,1)S(1)}, bf16[1024,640]{1,0:T(8,128)(2,1)}, u32[]{:S(2)}, u32[]{:S(2)}) collective-permute-start(bf16[1024,640]{1,0:T(8,128)(2,1)S(1)} %collective-permute-done.11.refs_8_.refs_4_), channel_id=1, source_target_pairs={{0,16},{1,17},{2,18},{3,19},{4,20},{5,21},{6,22},{7,23},{8,24},{9,... | collective-permute-start | bytes 3932168 | tf_op jit(solution)/shard_map/ppermute | solution.py:41
  57.8 18.7 %collective-permute-start.14 = (bf16[512,640]{1,0:T(8,128)(2,1)}, bf16[512,640]{1,0:T(8,128)(2,1)}, u32[]{:S(2)}, u32[]{:S(2)}) collective-permute-start(bf16[512,640]{1,0:T(8,128)(2,1)} %collective-permute-done.6.refs_5_), channel_id=1, source_target_pairs={{0,96},{1,97},{2,98},{3,99},{4,100},{5,101},{6,102},{7,103},{8,104... | collective-permute-start | bytes 1966088 | tf_op jit(solution)/shard_map/ppermute | solution.py:41
  57.9 18.6 %collective-permute-start.13 = (bf16[512,640]{1,0:T(8,128)(2,1)}, bf16[512,640]{1,0:T(8,128)(2,1)}, u32[]{:S(2)}, u32[]{:S(2)}) collective-permute-start(bf16[512,640]{1,0:T(8,128)(2,1)} %collective-permute-done.1.refs_1_), channel_id=1, source_target_pairs={{0,32},{1,33},{2,34},{3,35},{4,36},{5,37},{6,38},{7,39},{8,40},{9,... | collective-permute-start | bytes 1966088 | tf_op jit(solution)/shard_map/ppermute | solution.py:41
  61.8 1.1 copy-start.3
  85.0 2.0 %collective-permute-start.15 = (bf16[2,4,208,128]{3,2,1,0:T(8,128)(2,1)}, bf16[2,4,208,128]{3,2,1,0:T(8,128)(2,1)S(1)}, u32[]{:S(2)}, u32[]{:S(2)}) collective-permute-start(bf16[2,4,208,128]{3,2,1,0:T(8,128)(2,1)} %get-tuple-element.18), channel_id=1, source_target_pairs={{0,16},{1,17},{2,18},{3,19},{4,20},{5,21},{6,22},{7,23},{8,24},{9,... | collective-permute-start | bytes 1277960 | tf_op jit(solution)/shard_map/ppermute | solution.py:41
  87.0 5.5 %copy-start.1 = (bf16[2,4,208,128]{3,2,1,0:T(8,128)(2,1)S(1)}, bf16[2,4,208,128]{3,2,1,0:T(8,128)(2,1)}, u32[]{:S(2)}) copy-start(bf16[2,4,208,128]{3,2,1,0:T(8,128)(2,1)} %get-tuple-element.17) | copy-start | bytes 1277956
  88.2 12.4 %collective-permute-start.16 = (bf16[4,208,128]{2,1,0:T(8,128)(2,1)S(1)}, bf16[4,208,128]{2,1,0:T(8,128)(2,1)S(1)}, u32[]{:S(2)}, u32[]{:S(2)}) collective-permute-start(bf16[4,208,128]{2,1,0:T(8,128)(2,1)S(1)} %get-tuple-element.29), channel_id=1, source_target_pairs={{0,32},{1,33},{2,34},{3,35},{4,36},{5,37},{6,38},{7,39},{8,40},{9,... | collective-permute-start | bytes 638984 | tf_op jit(solution)/shard_map/ppermute | solution.py:41
  91.3 9.6 %collective-permute-start.17 = (bf16[4,208,128]{2,1,0:T(8,128)(2,1)S(1)}, bf16[4,208,128]{2,1,0:T(8,128)(2,1)S(1)}, u32[]{:S(2)}, u32[]{:S(2)}) collective-permute-start(bf16[4,208,128]{2,1,0:T(8,128)(2,1)S(1)} %get-tuple-element.28), channel_id=1, source_target_pairs={{0,64},{1,65},{2,66},{3,67},{4,68},{5,69},{6,70},{7,71},{8,72},{9,... | collective-permute-start | bytes 638984 | tf_op jit(solution)/shard_map/ppermute | solution.py:41
  91.3 12.8 %collective-permute-start.18 = (bf16[4,208,128]{2,1,0:T(8,128)(2,1)S(1)}, bf16[4,208,128]{2,1,0:T(8,128)(2,1)S(1)}, u32[]{:S(2)}, u32[]{:S(2)}) collective-permute-start(bf16[4,208,128]{2,1,0:T(8,128)(2,1)S(1)} %get-tuple-element.27), channel_id=1, source_target_pairs={{0,96},{1,97},{2,98},{3,99},{4,100},{5,101},{6,102},{7,103},{8,104... | collective-permute-start | bytes 638984 | tf_op jit(solution)/shard_map/ppermute | solution.py:41
where the time goes:
time: 141 us
  waiting for transfers between devices  60.3 us (43%)
  blocking collectives  34.8 us (25%)
  starting transfers between devices  20.3 us (14%)
  Pallas kernels  20.3 us (14%)
  local copies, waits for them, and re-layouts  2.96 us (2%)
  other arithmetic  2.17 us (2%)
    ppermute x19, waiting for transfers between devices, send(): return lax.ppermute(value, AXES, pairs(move))  60.3 us
    all_to_all x1, blocking collectives, local(): lax.all_to_all(pieces, 'owner', split_axis=0, concat_axis=0, tiled=True)  34.8 us
    ppermute x19, starting transfers between devices, send(): return lax.ppermute(value, AXES, pairs(move))  20.3 us
    pallas_call x1, Pallas kernels, accumulate(): pl.pallas_call(functools.partial(accumulate_kernel, plan, len(g_list), pr...  9.66 us
    pallas_call x1, Pallas kernels, finish(): pl.pallas_call(finish_kernel, grid_spec=pltpu.PrefetchScalarGridSpec(num_...  8.46 us
  transfers between devices with their start and end apart: 19, of which 13 were waited for; matrix products, arithmetic and copies ran while one was open for 1% of the time, Pallas kernels for 7%

commit v1 on v0

--- a/solution.py
+++ b/solution.py
@@ -21,7 +21,7 @@
 F32 = jnp.float32
 BF16 = jnp.bfloat16
 HI = lax.Precision.HIGHEST
-VMEM = 60 * 2**20
+VMEM = 28 * 2**20
 
 
 def params():
@@ -260,18 +260,14 @@
     g_left = send(columns(g_now, (x + 1) % 4, QUART), plus_x)
     g_right = send(columns(g_now, (x + 3) % 4, QUART), minus_x)
     g_far = send(columns(g_now, (x + 2) % 4, QUART), far_x)
-    mate = [
-        send(columns(a_now, 2 * (1 - y) + c, QUART), swap_y),
-        send(columns(a_now, 2 * (1 - y) + 1 - c, QUART), swap_y_core),
-    ]
-    own = [columns(a_now, 2 * y + c, QUART), send(columns(a_now, 2 * y + 1 - c, QUART), swap_core)]
-
-    own_all = jnp.concatenate(own, axis=0)
-    g_all = jnp.concatenate([columns(g_now, x, QUART), g_left, g_right, after(g_far, own_all)], axis=0)
-    g_mate = send(after(g_all, *mate), swap_y)
+    swapped = send(jnp.concatenate([columns(a_now, 2 * half + 1 - c, QUART) for half in (y, 1 - y)], axis=0), swap_core)
+    mate_all = send(jnp.concatenate([columns(a_now, 2 * (1 - y) + c, QUART), swapped[tok:]], axis=0), swap_y)
+    own_all = jnp.concatenate([columns(a_now, 2 * y + c, QUART), swapped[:tok]], axis=0)
+
+    g_all = jnp.concatenate([columns(g_now, x, QUART), g_left, g_right, g_far], axis=0)
+    g_mate = send(after(g_all, mate_all), swap_y)
     g_other = send(g_all, swap_core)
 
-    mate_all = jnp.concatenate(mate, axis=0)
     own_left, own_right = send(own_all, plus_x), send(own_all, minus_x)
     mate_left, mate_right = send(mate_all, plus_x), send(mate_all, minus_x)
     own_far = send(own_left, plus_x)

time: 141 us -> 132 us (0.936)
  Pallas kernels: 20.3 us -> 12.4 us
  waiting for transfers between devices: 60.3 us -> 66.2 us
  starting transfers between devices: 20.3 us -> 15.2 us
  other arithmetic: 2.17 us -> 0.52 us
    ppermute x19 -> x18, waiting for transfers between devices: 60.3 us -> 66.2 us  [send(): return lax.ppermute(value, AXES, pairs(move))]
    ppermute x19 -> x18, starting transfers between devices: 20.3 us -> 15.2 us  [send(): return lax.ppermute(value, AXES, pairs(move))]
    pallas_call x1, Pallas kernels: 9.66 us -> 6.02 us  [accumulate(): pl.pallas_call(functools.partial(accumulate_kernel, plan, len(g_list), pr...]
    pallas_call x1, Pallas kernels: 8.46 us -> 5.21 us  [finish(): pl.pallas_call(finish_kernel, grid_spec=pltpu.PrefetchScalarGridSpec(num_...]
  transfers between devices with their start and end apart: 19 -> 18, of which waited for: 13 -> 14; matrix products, arithmetic and copies ran while one was open for 1% -> 0% of each run, Pallas kernels for 7% -> 5%
where the time goes in v1:
time: 132 us
  waiting for transfers between devices  66.2 us (50%)
  blocking collectives  35.4 us (27%)
  starting transfers between devices  15.2 us (12%)
  Pallas kernels  12.4 us (9%)
  local copies, waits for them, and re-layouts  1.76 us (1%)
    ppermute x18, waiting for transfers between devices, send(): return lax.ppermute(value, AXES, pairs(move))  66.2 us
    all_to_all x1, blocking collectives, local(): lax.all_to_all(pieces, 'owner', split_axis=0, concat_axis=0, tiled=True)  35.4 us
    ppermute x18, starting transfers between devices, send(): return lax.ppermute(value, AXES, pairs(move))  15.2 us
    pallas_call x1, Pallas kernels, accumulate(): pl.pallas_call(functools.partial(accumulate_kernel, plan, len(g_list), pr...  6.02 us
    pallas_call x1, Pallas kernels, finish(): pl.pallas_call(finish_kernel, grid_spec=pltpu.PrefetchScalarGridSpec(num_...  5.21 us
  transfers between devices with their start and end apart: 18, of which 14 were waited for; matrix products, arithmetic and copies ran while one was open for 0% of the time, Pallas kernels for 5%

profile of v1, /device:TPU:38, one launch (start us, length us, event | category | flops | bytes accessed | tf_op | source)
XLA Modules:
  0.0 131.7 jit_solution(2024942044235722241)
XLA Ops:
  0.0 1.4 %dynamic-slice_bitcast_fusion.4 = (bf16[256,640]{1,0:T(8,128)(2,1)S(1)}, bf16[256,640]{1,0:T(8,128)(2,1)S(1)}, bf16[256,640]{1,0:T(8,128)(2,1)S(1)}, bf16[256,640]{1,0:T(8,128)(2,1)S(1)}) fusion(bf16[1,256,2560]{2,1,0:T(8,128)(2,1)} %param.2, s32[]{:T(128)S(6)} %select_n.187, s32[]{:T(128)S(6)} %select_n.185, s32[]{:T(128)S(6)} %select_n.184, s32[]{:T(128)S(6)} %select_n.186), kind=kLoop, calls=%fused_computation.8 | loop fusion | bytes 2621456 | tf_op jit(solution)/shard_map/dynamic_slice | solution.py:69
  1.4 0.1 pad_maximum_fusion.1
  1.5 0.0 copy-start
  1.5 0.1 collective-permute-start
  1.6 2.1 %collective-permute-done = bf16[512,640]{1,0:T(8,128)(2,1)S(1)} collective-permute-done((bf16[512,640]{1,0:T(8,128)(2,1)S(1)}, bf16[512,640]{1,0:T(8,128)(2,1)S(1)}, u32[]{:S(2)}, u32[]{:S(2)}) %collective-permute-start) | collective-permute-done | bytes 655392 | tf_op jit(solution)/shard_map/ppermute | solution.py:41
  3.7 0.1 fusion
  3.7 0.1 pad_maximum_fusion.3
  3.8 1.7 %collective-permute-start.3 = (bf16[512,640]{1,0:T(8,128)(2,1)S(1)}, bf16[512,640]{1,0:T(8,128)(2,1)S(1)}, u32[]{:S(2)}, u32[]{:S(2)}) collective-permute-start(bf16[512,640]{1,0:T(8,128)(2,1)S(1)} %pad_maximum_fusion.3), channel_id=1, source_target_pairs={{0,128},{1,129},{2,130},{3,131},{4,132},{5,133},{6,134},{7,135},{8... | collective-permute-start | bytes 1966088 | tf_op jit(solution)/shard_map/ppermute | solution.py:41
  5.4 0.1 dynamic-slice_bitcast_fusion.3
  5.6 0.6 collective-permute-start.6
  6.1 1.5 %collective-permute-start.7 = (bf16[256,640]{1,0:T(8,128)(2,1)S(1)}, bf16[256,640]{1,0:T(8,128)(2,1)S(1)}, u32[]{:S(2)}, u32[]{:S(2)}) collective-permute-start(bf16[256,640]{1,0:T(8,128)(2,1)S(1)} %get-tuple-element.20), channel_id=1, source_target_pairs={{0,96},{1,97},{2,98},{3,99},{4,100},{5,101},{6,102},{7,103},{8,104... | collective-permute-start | bytes 983048 | tf_op jit(solution)/shard_map/ppermute | solution.py:41
  7.7 1.4 %collective-permute-start.8 = (bf16[256,640]{1,0:T(8,128)(2,1)S(1)}, bf16[256,640]{1,0:T(8,128)(2,1)S(1)}, u32[]{:S(2)}, u32[]{:S(2)}) collective-permute-start(bf16[256,640]{1,0:T(8,128)(2,1)S(1)} %get-tuple-element.19), channel_id=1, source_target_pairs={{0,64},{1,65},{2,66},{3,67},{4,68},{5,69},{6,70},{7,71},{8,72},{9,... | collective-permute-start | bytes 983048 | tf_op jit(solution)/shard_map/ppermute | solution.py:41
  9.1 7.2 %collective-permute-done.6 = bf16[256,640]{1,0:T(8,128)(2,1)S(1)} collective-permute-done((bf16[256,640]{1,0:T(8,128)(2,1)S(1)}, bf16[256,640]{1,0:T(8,128)(2,1)S(1)}, u32[]{:S(2)}, u32[]{:S(2)}) %collective-permute-start.6) | collective-permute-done | bytes 327712 | tf_op jit(solution)/shard_map/ppermute | solution.py:41
  16.2 7.3 %collective-permute-done.7 = bf16[256,640]{1,0:T(8,128)(2,1)S(1)} collective-permute-done((bf16[256,640]{1,0:T(8,128)(2,1)S(1)}, bf16[256,640]{1,0:T(8,128)(2,1)S(1)}, u32[]{:S(2)}, u32[]{:S(2)}) %collective-permute-start.7) | collective-permute-done | bytes 327712 | tf_op jit(solution)/shard_map/ppermute | solution.py:41
  23.5 0.0 collective-permute-done.8
  23.6 0.1 pad_maximum_fusion.refs_6_.refs_2_
  23.7 0.0 collective-permute-done.3.refs_3_
  23.7 0.5 collective-permute-start.10
  24.2 0.1 pad_maximum_fusion.2.refs_0_
  24.3 1.3 %collective-permute-start.1 = (bf16[512,640]{1,0:T(8,128)(2,1)S(1)}, bf16[512,640]{1,0:T(8,128)(2,1)S(1)}, u32[]{:S(2)}, u32[]{:S(2)}) collective-permute-start(bf16[512,640]{1,0:T(8,128)(2,1)S(1)} %pad_maximum_fusion.2.refs_0_), channel_id=1, source_target_pairs={{0,32},{1,33},{2,34},{3,35},{4,36},{5,37},{6,38},{7,39},{8,40},{9,... | collective-permute-start | bytes 1966088 | tf_op jit(solution)/shard_map/ppermute | solution.py:41
  25.6 0.8 collective-permute-start.2
  26.4 2.5 %collective-permute-start.4 = (bf16[512,640]{1,0:T(8,128)(2,1)S(1)}, bf16[512,640]{1,0:T(8,128)(2,1)S(1)}, u32[]{:S(2)}, u32[]{:S(2)}) collective-permute-start(bf16[512,640]{1,0:T(8,128)(2,1)S(1)} %collective-permute-done.3.refs_3_), channel_id=1, source_target_pairs={{0,32},{1,33},{2,34},{3,35},{4,36},{5,37},{6,38},{7,39},{8,40},{9,... | collective-permute-start | bytes 1966088 | tf_op jit(solution)/shard_map/ppermute | solution.py:41
  28.9 13.2 %collective-permute-done.1.refs_1_ = bf16[512,640]{1,0:T(8,128)(2,1)S(1)} collective-permute-done((bf16[512,640]{1,0:T(8,128)(2,1)S(1)}, bf16[512,640]{1,0:T(8,128)(2,1)S(1)}, u32[]{:S(2)}, u32[]{:S(2)}) %collective-permute-start.1) | collective-permute-done | bytes 655392 | tf_op jit(solution)/shard_map/ppermute | solution.py:41
  42.0 2.5 %collective-permute-done.2.refs_2_ = bf16[512,640]{1,0:T(8,128)(2,1)S(1)} collective-permute-done((bf16[512,640]{1,0:T(8,128)(2,1)S(1)}, bf16[512,640]{1,0:T(8,128)(2,1)S(1)}, u32[]{:S(2)}, u32[]{:S(2)}) %collective-permute-start.2) | collective-permute-done | bytes 655392 | tf_op jit(solution)/shard_map/ppermute | solution.py:41
  44.5 8.7 %collective-permute-done.4.refs_4_ = bf16[512,640]{1,0:T(8,128)(2,1)S(1)} collective-permute-done((bf16[512,640]{1,0:T(8,128)(2,1)S(1)}, bf16[512,640]{1,0:T(8,128)(2,1)S(1)}, u32[]{:S(2)}, u32[]{:S(2)}) %collective-permute-start.4) | collective-permute-done | bytes 655392 | tf_op jit(solution)/shard_map/ppermute | solution.py:41
  53.2 2.8 %collective-permute-done.5.refs_5_ = bf16[512,640]{1,0:T(8,128)(2,1)S(1)} collective-permute-done((bf16[512,640]{1,0:T(8,128)(2,1)S(1)}, bf16[512,640]{1,0:T(8,128)(2,1)S(1)}, u32[]{:S(2)}, u32[]{:S(2)}) %collective-permute-start.5) | collective-permute-done | bytes 655392 | tf_op jit(solution)/shard_map/ppermute | solution.py:41
  55.9 0.0 collective-permute-done.10.refs_8_.refs_4_
  55.9 0.4 collective-permute-start.12
  56.3 1.7 %collective-permute-start.13 = (bf16[512,640]{1,0:T(8,128)(2,1)S(1)}, bf16[512,640]{1,0:T(8,128)(2,1)S(1)}, u32[]{:S(2)}, u32[]{:S(2)}) collective-permute-start(bf16[512,640]{1,0:T(8,128)(2,1)S(1)} %collective-permute-done.5.refs_5_), channel_id=1, source_target_pairs={{0,96},{1,97},{2,98},{3,99},{4,100},{5,101},{6,102},{7,103},{8,104... | collective-permute-start | bytes 1966088 | tf_op jit(solution)/shard_map/ppermute | solution.py:41
  58.0 0.1 pad_add_fusion.core
  58.0 0.0 collective-permute-done.9.refs_7_.refs_3_
  58.0 0.9 collective-permute-done.11.refs_9_.refs_5_
  59.0 6.0 %accumulate.1 = (f32[640,640]{1,0:T(8,128)S(1)}, f32[5,2,128,128]{3,2,1,0:T(8,128)S(1)}) custom-call(bf16[512,640]{1,0:T(8,128)(2,1)S(1)} %pad_maximum_fusion.2.refs_0_, bf16[512,640]{1,0:T(8,128)(2,1)S(1)} %collective-permute-done.1.refs_1_, bf16[512,640]{1,0:T(8,128)(2,1)S(1)} %collective-permute-done.2.refs_2_, ...), custom_call_target="tpu_custom_call" | custom-call | flops 3523215360 | bytes 11141120 | tf_op jit(solution)/shard_map/accumulate/pallas_call | solution.py:106
  65.0 8.1 %collective-permute-done.12.refs_0_ = bf16[512,640]{1,0:T(8,128)(2,1)S(1)} collective-permute-done((bf16[512,640]{1,0:T(8,128)(2,1)S(1)}, bf16[512,640]{1,0:T(8,128)(2,1)S(1)}, u32[]{:S(2)}, u32[]{:S(2)}) %collective-permute-start.12) | collective-permute-done | bytes 655392 | tf_op jit(solution)/shard_map/ppermute | solution.py:41
  73.1 1.2 collective-permute-done.13.refs_1_
  74.3 5.2 %finish.1 = (bf16[2,4,208,128]{3,2,1,0:T(8,128)(2,1)S(1)}, bf16[2,4,208,128]{3,2,1,0:T(8,128)(2,1)S(1)}) custom-call(s32[2]{0:T(128)S(1)} %pad_add_fusion.core, f32[640,640]{1,0:T(8,128)S(1)} %get-tuple-element.13.s_prev, f32[5,2,128,128]{3,2,1,0:T(8,128)S(1)} %get-tuple-element.14.m_prev, bf16[512,640]{1,0:T(8,128)(2,1)S(1)} %collective-permute-done.12.refs_0_, ...), custom_call_target="tpu_custom_call" | custom-call | flops 2000000000 | bytes 5000000 | tf_op jit(solution)/shard_map/finish/pallas_call | solution.py:213
  79.5 0.1 collective-permute-start.14
  79.7 1.6 %collective-permute-done.14 = bf16[2,4,208,128]{3,2,1,0:T(8,128)(2,1)S(1)} collective-permute-done((bf16[2,4,208,128]{3,2,1,0:T(8,128)(2,1)S(1)}, bf16[2,4,208,128]{3,2,1,0:T(8,128)(2,1)S(1)}, u32[]{:S(2)}, u32[]{:S(2)}) %collective-permute-start.14) | collective-permute-done | bytes 426016 | tf_op jit(solution)/shard_map/ppermute | solution.py:41
  81.4 0.1 select_bitcast_fusion
  81.5 0.4 collective-permute-start.15
  81.8 2.3 %collective-permute-start.16 = (bf16[4,208,128]{2,1,0:T(8,128)(2,1)S(1)}, bf16[4,208,128]{2,1,0:T(8,128)(2,1)S(1)}, u32[]{:S(2)}, u32[]{:S(2)}) collective-permute-start(bf16[4,208,128]{2,1,0:T(8,128)(2,1)S(1)} %get-tuple-element.26), channel_id=1, source_target_pairs={{0,64},{1,65},{2,66},{3,67},{4,68},{5,69},{6,70},{7,71},{8,72},{9,... | collective-permute-start | bytes 638984 | tf_op jit(solution)/shard_map/ppermute | solution.py:41
  84.1 0.1 broadcast_in_dim.3
  84.2 0.1 bitcast_dynamic-update-slice_fusion
  84.3 5.3 %collective-permute-done.15 = bf16[4,208,128]{2,1,0:T(8,128)(2,1)S(1)} collective-permute-done((bf16[4,208,128]{2,1,0:T(8,128)(2,1)S(1)}, bf16[4,208,128]{2,1,0:T(8,128)(2,1)S(1)}, u32[]{:S(2)}, u32[]{:S(2)}) %collective-permute-start.15) | collective-permute-done | bytes 213024 | tf_op jit(solution)/shard_map/ppermute | solution.py:41
  89.7 1.8 %collective-permute-done.16 = bf16[4,208,128]{2,1,0:T(8,128)(2,1)S(1)} collective-permute-done((bf16[4,208,128]{2,1,0:T(8,128)(2,1)S(1)}, bf16[4,208,128]{2,1,0:T(8,128)(2,1)S(1)}, u32[]{:S(2)}, u32[]{:S(2)}) %collective-permute-start.16) | collective-permute-done | bytes 213024 | tf_op jit(solution)/shard_map/ppermute | solution.py:41
  91.5 3.6 %collective-permute-done.17 = bf16[4,208,128]{2,1,0:T(8,128)(2,1)S(1)} collective-permute-done((bf16[4,208,128]{2,1,0:T(8,128)(2,1)S(1)}, bf16[4,208,128]{2,1,0:T(8,128)(2,1)S(1)}, u32[]{:S(2)}, u32[]{:S(2)}) %collective-permute-start.17) | collective-permute-done | bytes 213024 | tf_op jit(solution)/shard_map/ppermute | solution.py:41
  95.1 35.4 %all_to_all.5.src = bf16[16,208,128]{2,1,0:T(8,128)(2,1)S(1)} all-to-all(bf16[16,208,128]{2,1,0:T(8,128)(2,1)S(1)} %constant_dynamic-update-slice_fusion.2), channel_id=1, replica_groups=mesh['dp'=16,'owner'=16] {'owner'}, dimensions={0} | all-to-all | bytes 1703936 | tf_op jit(solution)/shard_map/all_to_all | solution.py:294
  130.5 1.2 unpack.1
  (8 shorter events, 0.1 us)
Async XLA Ops:
  1.5 4.0 %copy-start = (bf16[1,256,2560]{2,1,0:T(8,128)(2,1)S(1)}, bf16[1,256,2560]{2,1,0:T(8,128)(2,1)}, u32[]{:S(2)}) copy-start(bf16[1,256,2560]{2,1,0:T(8,128)(2,1)} %param.3) | copy-start | bytes 3932164
  1.5 2.2 %collective-permute-start = (bf16[512,640]{1,0:T(8,128)(2,1)S(1)}, bf16[512,640]{1,0:T(8,128)(2,1)S(1)}, u32[]{:S(2)}, u32[]{:S(2)}) collective-permute-start(bf16[512,640]{1,0:T(8,128)(2,1)S(1)} %pad_maximum_fusion.1), channel_id=1, source_target_pairs={{0,16},{1,17},{2,18},{3,19},{4,20},{5,21},{6,22},{7,23},{8,24},{9,... | collective-permute-start | bytes 1966088 | tf_op jit(solution)/shard_map/ppermute | solution.py:41
  3.8 19.9 %collective-permute-start.3 = (bf16[512,640]{1,0:T(8,128)(2,1)S(1)}, bf16[512,640]{1,0:T(8,128)(2,1)S(1)}, u32[]{:S(2)}, u32[]{:S(2)}) collective-permute-start(bf16[512,640]{1,0:T(8,128)(2,1)S(1)} %pad_maximum_fusion.3), channel_id=1, source_target_pairs={{0,128},{1,129},{2,130},{3,131},{4,132},{5,133},{6,134},{7,135},{8... | collective-permute-start | bytes 1966088 | tf_op jit(solution)/shard_map/ppermute | solution.py:41
  5.6 10.7 %collective-permute-start.6 = (bf16[256,640]{1,0:T(8,128)(2,1)S(1)}, bf16[256,640]{1,0:T(8,128)(2,1)S(1)}, u32[]{:S(2)}, u32[]{:S(2)}) collective-permute-start(bf16[256,640]{1,0:T(8,128)(2,1)S(1)} %get-tuple-element.18), channel_id=1, source_target_pairs={{0,32},{1,33},{2,34},{3,35},{4,36},{5,37},{6,38},{7,39},{8,40},{9,... | collective-permute-start | bytes 983048 | tf_op jit(solution)/shard_map/ppermute | solution.py:41
  6.1 17.4 %collective-permute-start.7 = (bf16[256,640]{1,0:T(8,128)(2,1)S(1)}, bf16[256,640]{1,0:T(8,128)(2,1)S(1)}, u32[]{:S(2)}, u32[]{:S(2)}) collective-permute-start(bf16[256,640]{1,0:T(8,128)(2,1)S(1)} %get-tuple-element.20), channel_id=1, source_target_pairs={{0,96},{1,97},{2,98},{3,99},{4,100},{5,101},{6,102},{7,103},{8,104... | collective-permute-start | bytes 983048 | tf_op jit(solution)/shard_map/ppermute | solution.py:41
  7.7 15.9 %collective-permute-start.8 = (bf16[256,640]{1,0:T(8,128)(2,1)S(1)}, bf16[256,640]{1,0:T(8,128)(2,1)S(1)}, u32[]{:S(2)}, u32[]{:S(2)}) collective-permute-start(bf16[256,640]{1,0:T(8,128)(2,1)S(1)} %get-tuple-element.19), channel_id=1, source_target_pairs={{0,64},{1,65},{2,66},{3,67},{4,68},{5,69},{6,70},{7,71},{8,72},{9,... | collective-permute-start | bytes 983048 | tf_op jit(solution)/shard_map/ppermute | solution.py:41
  23.7 32.3 %collective-permute-start.10 = (bf16[1024,640]{1,0:T(8,128)(2,1)S(1)}, bf16[1024,640]{1,0:T(8,128)(2,1)S(1)}, u32[]{:S(2)}, u32[]{:S(2)}) collective-permute-start(bf16[1024,640]{1,0:T(8,128)(2,1)S(1)} %pad_maximum_fusion.refs_6_.refs_2_), channel_id=1, source_target_pairs={{0,128},{1,129},{2,130},{3,131},{4,132},{5,133},{6,134},{7,135},{8... | collective-permute-start | bytes 3932168 | tf_op jit(solution)/shard_map/ppermute | solution.py:41
  24.3 17.7 %collective-permute-start.1 = (bf16[512,640]{1,0:T(8,128)(2,1)S(1)}, bf16[512,640]{1,0:T(8,128)(2,1)S(1)}, u32[]{:S(2)}, u32[]{:S(2)}) collective-permute-start(bf16[512,640]{1,0:T(8,128)(2,1)S(1)} %pad_maximum_fusion.2.refs_0_), channel_id=1, source_target_pairs={{0,32},{1,33},{2,34},{3,35},{4,36},{5,37},{6,38},{7,39},{8,40},{9,... | collective-permute-start | bytes 1966088 | tf_op jit(solution)/shard_map/ppermute | solution.py:41
  25.6 18.9 %collective-permute-start.2 = (bf16[512,640]{1,0:T(8,128)(2,1)S(1)}, bf16[512,640]{1,0:T(8,128)(2,1)S(1)}, u32[]{:S(2)}, u32[]{:S(2)}) collective-permute-start(bf16[512,640]{1,0:T(8,128)(2,1)S(1)} %pad_maximum_fusion.2.refs_0_), channel_id=1, source_target_pairs={{0,96},{1,97},{2,98},{3,99},{4,100},{5,101},{6,102},{7,103},{8,104... | collective-permute-start | bytes 1966088 | tf_op jit(solution)/shard_map/ppermute | solution.py:41
  26.4 26.8 %collective-permute-start.4 = (bf16[512,640]{1,0:T(8,128)(2,1)S(1)}, bf16[512,640]{1,0:T(8,128)(2,1)S(1)}, u32[]{:S(2)}, u32[]{:S(2)}) collective-permute-start(bf16[512,640]{1,0:T(8,128)(2,1)S(1)} %collective-permute-done.3.refs_3_), channel_id=1, source_target_pairs={{0,32},{1,33},{2,34},{3,35},{4,36},{5,37},{6,38},{7,39},{8,40},{9,... | collective-permute-start | bytes 1966088 | tf_op jit(solution)/shard_map/ppermute | solution.py:41
  28.9 27.1 %collective-permute-start.5 = (bf16[512,640]{1,0:T(8,128)(2,1)S(1)}, bf16[512,640]{1,0:T(8,128)(2,1)S(1)}, u32[]{:S(2)}, u32[]{:S(2)}) collective-permute-start(bf16[512,640]{1,0:T(8,128)(2,1)S(1)} %collective-permute-done.3.refs_3_), channel_id=1, source_target_pairs={{0,96},{1,97},{2,98},{3,99},{4,100},{5,101},{6,102},{7,103},{8,104... | collective-permute-start | bytes 1966088 | tf_op jit(solution)/shard_map/ppermute | solution.py:41
  42.0 16.0 %collective-permute-start.9 = (bf16[1024,640]{1,0:T(8,128)(2,1)S(1)}, bf16[1024,640]{1,0:T(8,128)(2,1)S(1)}, u32[]{:S(2)}, u32[]{:S(2)}) collective-permute-start(bf16[1024,640]{1,0:T(8,128)(2,1)S(1)} %pad_maximum_fusion.refs_6_.refs_2_), channel_id=1, source_target_pairs={{0,16},{1,17},{2,18},{3,19},{4,20},{5,21},{6,22},{7,23},{8,24},{9,... | collective-permute-start | bytes 3932168 | tf_op jit(solution)/shard_map/ppermute | solution.py:41
  55.9 3.0 %collective-permute-start.11 = (bf16[1024,640]{1,0:T(8,128)(2,1)S(1)}, bf16[1024,640]{1,0:T(8,128)(2,1)S(1)}, u32[]{:S(2)}, u32[]{:S(2)}) collective-permute-start(bf16[1024,640]{1,0:T(8,128)(2,1)S(1)} %collective-permute-done.10.refs_8_.refs_4_), channel_id=1, source_target_pairs={{0,16},{1,17},{2,18},{3,19},{4,20},{5,21},{6,22},{7,23},{8,24},{9,... | collective-permute-start | bytes 3932168 | tf_op jit(solution)/shard_map/ppermute | solution.py:41
  55.9 17.1 %collective-permute-start.12 = (bf16[512,640]{1,0:T(8,128)(2,1)S(1)}, bf16[512,640]{1,0:T(8,128)(2,1)S(1)}, u32[]{:S(2)}, u32[]{:S(2)}) collective-permute-start(bf16[512,640]{1,0:T(8,128)(2,1)S(1)} %collective-permute-done.1.refs_1_), channel_id=1, source_target_pairs={{0,32},{1,33},{2,34},{3,35},{4,36},{5,37},{6,38},{7,39},{8,40},{9,... | collective-permute-start | bytes 1966088 | tf_op jit(solution)/shard_map/ppermute | solution.py:41
  56.3 18.0 %collective-permute-start.13 = (bf16[512,640]{1,0:T(8,128)(2,1)S(1)}, bf16[512,640]{1,0:T(8,128)(2,1)S(1)}, u32[]{:S(2)}, u32[]{:S(2)}) collective-permute-start(bf16[512,640]{1,0:T(8,128)(2,1)S(1)} %collective-permute-done.5.refs_5_), channel_id=1, source_target_pairs={{0,96},{1,97},{2,98},{3,99},{4,100},{5,101},{6,102},{7,103},{8,104... | collective-permute-start | bytes 1966088 | tf_op jit(solution)/shard_map/ppermute | solution.py:41
  79.5 1.9 %collective-permute-start.14 = (bf16[2,4,208,128]{3,2,1,0:T(8,128)(2,1)S(1)}, bf16[2,4,208,128]{3,2,1,0:T(8,128)(2,1)S(1)}, u32[]{:S(2)}, u32[]{:S(2)}) collective-permute-start(bf16[2,4,208,128]{3,2,1,0:T(8,128)(2,1)S(1)} %get-tuple-element.16), channel_id=1, source_target_pairs={{0,16},{1,17},{2,18},{3,19},{4,20},{5,21},{6,22},{7,23},{8,24},{9,... | collective-permute-start | bytes 1277960 | tf_op jit(solution)/shard_map/ppermute | solution.py:41
  81.5 8.2 %collective-permute-start.15 = (bf16[4,208,128]{2,1,0:T(8,128)(2,1)S(1)}, bf16[4,208,128]{2,1,0:T(8,128)(2,1)S(1)}, u32[]{:S(2)}, u32[]{:S(2)}) collective-permute-start(bf16[4,208,128]{2,1,0:T(8,128)(2,1)S(1)} %get-tuple-element.27), channel_id=1, source_target_pairs={{0,32},{1,33},{2,34},{3,35},{4,36},{5,37},{6,38},{7,39},{8,40},{9,... | collective-permute-start | bytes 638984 | tf_op jit(solution)/shard_map/ppermute | solution.py:41
  81.8 9.7 %collective-permute-start.16 = (bf16[4,208,128]{2,1,0:T(8,128)(2,1)S(1)}, bf16[4,208,128]{2,1,0:T(8,128)(2,1)S(1)}, u32[]{:S(2)}, u32[]{:S(2)}) collective-permute-start(bf16[4,208,128]{2,1,0:T(8,128)(2,1)S(1)} %get-tuple-element.26), channel_id=1, source_target_pairs={{0,64},{1,65},{2,66},{3,67},{4,68},{5,69},{6,70},{7,71},{8,72},{9,... | collective-permute-start | bytes 638984 | tf_op jit(solution)/shard_map/ppermute | solution.py:41
  84.1 11.0 %collective-permute-start.17 = (bf16[4,208,128]{2,1,0:T(8,128)(2,1)S(1)}, bf16[4,208,128]{2,1,0:T(8,128)(2,1)S(1)}, u32[]{:S(2)}, u32[]{:S(2)}) collective-permute-start(bf16[4,208,128]{2,1,0:T(8,128)(2,1)S(1)} %get-tuple-element.25), channel_id=1, source_target_pairs={{0,96},{1,97},{2,98},{3,99},{4,100},{5,101},{6,102},{7,103},{8,104... | collective-permute-start | bytes 638984 | tf_op jit(solution)/shard_map/ppermute | solution.py:41

commit v2 on v1

--- a/solution.py
+++ b/solution.py
@@ -215,7 +215,7 @@
         grid_spec=pltpu.PrefetchScalarGridSpec(
             num_scalar_prefetch=1,
             grid=(1,),
-            in_specs=[whole(v.shape) for v in (*sums, *a_late)] + [pl.BlockSpec((tok, QUART), lambda i, c: (3, 0))] * 4,
+            in_specs=[whole(v.shape) for v in (*sums, *a_late)] + [whole((tok, QUART))] * 4,
             out_specs=[whole(out.shape)] * 2,
             scratch_shapes=[pltpu.VMEM((2 * NB, BLK, BLK), F32), pltpu.VMEM((QUART, QUART), F32)],
         ),
@@ -260,27 +260,33 @@
     g_left = send(columns(g_now, (x + 1) % 4, QUART), plus_x)
     g_right = send(columns(g_now, (x + 3) % 4, QUART), minus_x)
     g_far = send(columns(g_now, (x + 2) % 4, QUART), far_x)
-    swapped = send(jnp.concatenate([columns(a_now, 2 * half + 1 - c, QUART) for half in (y, 1 - y)], axis=0), swap_core)
-    mate_all = send(jnp.concatenate([columns(a_now, 2 * (1 - y) + c, QUART), swapped[tok:]], axis=0), swap_y)
-    own_all = jnp.concatenate([columns(a_now, 2 * y + c, QUART), swapped[:tok]], axis=0)
-
-    g_all = jnp.concatenate([columns(g_now, x, QUART), g_left, g_right, g_far], axis=0)
-    g_mate = send(after(g_all, mate_all), swap_y)
-    g_other = send(g_all, swap_core)
-
+    mate_all = jnp.concatenate(
+        [send(columns(a_now, 2 * (1 - y) + c, QUART), swap_y), send(columns(a_now, 2 * (1 - y) + 1 - c, QUART), swap_y_core)], axis=0
+    )
+    own_all = jnp.concatenate(
+        [columns(a_now, 2 * y + c, QUART), send(columns(a_now, 2 * y + 1 - c, QUART), swap_core)], axis=0
+    )
+    g_near = jnp.concatenate([columns(g_now, x, QUART), g_left, g_right], axis=0)
+    g_mate = send(after(g_near, mate_all), swap_y)
+    g_other = send(g_near, swap_core)
     own_left, own_right = send(own_all, plus_x), send(own_all, minus_x)
-    mate_left, mate_right = send(mate_all, plus_x), send(mate_all, minus_x)
+    mate_start = after(mate_all, g_far)
+    mate_left, mate_right = send(mate_start, plus_x), send(mate_start, minus_x)
+    g_far_mate = send(after(g_far, own_left, own_right), swap_y)
     own_far = send(own_left, plus_x)
     mate_far = send(mate_right, minus_x)
     g_mate_other = send(after(g_mate, own_left, own_right, mate_left, mate_right), swap_core)
     plan = [[(n, k * tok, tok), (n + 1, k * tok, tok)] for n in (0, 2) for k in range(3)]
     sums = accumulate(
-        [own_all, own_left, own_right, mate_all, mate_left, mate_right], plan, [g_all, g_other, g_mate, g_mate_other]
-    )
-    keep, give = finish(place, sums, [own_far, mate_far], [g_all, g_other, g_mate, g_mate_other])
+        [own_all, own_left, own_right, mate_all, mate_left, mate_right], plan, [g_near, g_other, g_mate, g_mate_other]
+    )
+    g_late = []
+    for block in lax.optimization_barrier((g_far, g_far_mate, mate_left, mate_right))[:2]:
+        g_late += [block, send(block, swap_core)]
+    keep, give = finish(place, sums, [own_far, mate_far], g_late)
     recv = send(give, swap_core)
     got = []
-    for k, move in enumerate([None, plus_x, far_x, minus_x]):
+    for k, move in ((0, None), (1, plus_x), (3, minus_x), (2, far_x)):
         target = (x + k) % 4
         strip = jnp.where(
             target // 2 == c,
@@ -289,8 +295,8 @@
         )
         got.append(strip if move is None else send(strip, move))
     pieces = jnp.zeros((16, PACK, BLK), BF16)
-    for k in range(4):
-        pieces = lax.dynamic_update_slice(pieces, got[k], (((x + 4 - k) % 4) * 4, 0, 0))
+    for k, strip in zip((0, 1, 3, 2), got):
+        pieces = lax.dynamic_update_slice(pieces, strip, (((x + 4 - k) % 4) * 4, 0, 0))
     return unpack(lax.all_to_all(pieces, "owner", split_axis=0, concat_axis=0, tiled=True))
 
 

time: 132 us -> 130 us (0.985)
  waiting for transfers between devices: 66.2 us -> 60.7 us
  starting transfers between devices: 15.2 us -> 19.3 us
  blocking collectives: 35.4 us -> 33.7 us
    ppermute x18 -> x22, waiting for transfers between devices: 66.2 us -> 60.7 us  [send(): return lax.ppermute(value, AXES, pairs(move))]
    ppermute x18 -> x22, starting transfers between devices: 15.2 us -> 19.3 us  [send(): return lax.ppermute(value, AXES, pairs(move))]
    all_to_all x1, blocking collectives: 35.4 us -> 33.7 us  [local(): lax.all_to_all(pieces, 'owner', split_axis=0, concat_axis=0, tiled=True)]
  transfers between devices with their start and end apart: 18 -> 22, of which waited for: 14 -> 13; matrix products, arithmetic and copies ran while one was open for 0% -> 1% of each run, Pallas kernels for 5% -> 5%
where the time goes in v2:
time: 130 us; the launch traced here: 129 us
  waiting for transfers between devices  60.7 us (47%)
  blocking collectives  33.7 us (26%)
  starting transfers between devices  19.3 us (15%)
  Pallas kernels  12.4 us (10%)
  local copies, waits for them, and re-layouts  1.88 us (1%)
    ppermute x22, waiting for transfers between devices, send(): return lax.ppermute(value, AXES, pairs(move))  60.7 us
    all_to_all x1, blocking collectives, local(): lax.all_to_all(pieces, 'owner', split_axis=0, concat_axis=0, tiled=True)  33.7 us
    ppermute x22, starting transfers between devices, send(): return lax.ppermute(value, AXES, pairs(move))  19.3 us
    pallas_call x1, Pallas kernels, accumulate(): pl.pallas_call(functools.partial(accumulate_kernel, plan, len(g_list), pr...  6.03 us
    pallas_call x1, Pallas kernels, finish(): pl.pallas_call(finish_kernel, grid_spec=pltpu.PrefetchScalarGridSpec(num_...  5.14 us
  transfers between devices with their start and end apart: 22, of which 13 were waited for; matrix products, arithmetic and copies ran while one was open for 1% of the time, Pallas kernels for 5%

profile of v2, /device:TPU:38, one launch (start us, length us, event | category | flops | bytes accessed | tf_op | source)
XLA Modules:
  0.0 128.5 jit_solution(14035943366561477730)
XLA Ops:
  0.0 1.5 %dynamic-slice_bitcast_fusion.2 = (bf16[256,640]{1,0:T(8,128)(2,1)S(1)}, bf16[256,640]{1,0:T(8,128)(2,1)S(1)}, bf16[256,640]{1,0:T(8,128)(2,1)S(1)}, bf16[256,640]{1,0:T(8,128)(2,1)S(1)}) fusion(bf16[1,256,2560]{2,1,0:T(8,128)(2,1)} %param.3, s32[]{:T(128)S(6)} %select_n.190, s32[]{:T(128)S(6)} %select_n.189, s32[]{:T(128)S(6)} %select_n.194, s32[]{:T(128)S(6)} %select_n.192), kind=kLoop, calls=%fused_computation.4 | loop fusion | bytes 2621456 | tf_op jit(solution)/shard_map/dynamic_slice | solution.py:69
  1.5 0.9 collective-permute-start.9
  2.4 2.4 %collective-permute-start.8 = (bf16[256,640]{1,0:T(8,128)(2,1)S(1)}, bf16[256,640]{1,0:T(8,128)(2,1)S(1)}, u32[]{:S(2)}, u32[]{:S(2)}) collective-permute-start(bf16[256,640]{1,0:T(8,128)(2,1)S(1)} %get-tuple-element.28), channel_id=1, source_target_pairs={{0,32},{1,33},{2,34},{3,35},{4,36},{5,37},{6,38},{7,39},{8,40},{9,... | collective-permute-start | bytes 983048 | tf_op jit(solution)/shard_map/ppermute | solution.py:41
  4.8 0.1 dynamic-slice_bitcast_fusion.4
  4.9 1.7 %collective-permute-start.3 = (bf16[256,640]{1,0:T(8,128)(2,1)S(1)}, bf16[256,640]{1,0:T(8,128)(2,1)S(1)}, u32[]{:S(2)}, u32[]{:S(2)}) collective-permute-start(bf16[256,640]{1,0:T(8,128)(2,1)S(1)} %get-tuple-element.32), channel_id=1, source_target_pairs={{0,128},{1,129},{2,130},{3,131},{4,132},{5,133},{6,134},{7,135},{8... | collective-permute-start | bytes 983048 | tf_op jit(solution)/shard_map/ppermute | solution.py:41
  6.6 0.6 collective-permute-start
  7.2 5.1 %collective-permute-done.9 = bf16[256,640]{1,0:T(8,128)(2,1)S(1)} collective-permute-done((bf16[256,640]{1,0:T(8,128)(2,1)S(1)}, bf16[256,640]{1,0:T(8,128)(2,1)S(1)}, u32[]{:S(2)}, u32[]{:S(2)}) %collective-permute-start.9) | collective-permute-done | bytes 327712 | tf_op jit(solution)/shard_map/ppermute | solution.py:41
  12.2 0.2 collective-permute-start.5
  12.4 6.1 %collective-permute-done.8 = bf16[256,640]{1,0:T(8,128)(2,1)S(1)} collective-permute-done((bf16[256,640]{1,0:T(8,128)(2,1)S(1)}, bf16[256,640]{1,0:T(8,128)(2,1)S(1)}, u32[]{:S(2)}, u32[]{:S(2)}) %collective-permute-start.8) | collective-permute-done | bytes 327712 | tf_op jit(solution)/shard_map/ppermute | solution.py:41
  18.6 0.1 pad_maximum_fusion.refs_6_
  18.7 1.3 %collective-permute-done.4 = bf16[256,640]{1,0:T(8,128)(2,1)S(1)} collective-permute-done((bf16[256,640]{1,0:T(8,128)(2,1)S(1)}, bf16[256,640]{1,0:T(8,128)(2,1)S(1)}, u32[]{:S(2)}, u32[]{:S(2)}) %collective-permute-start.4) | collective-permute-done | bytes 327712 | tf_op jit(solution)/shard_map/ppermute | solution.py:41
  20.1 0.8 collective-permute-start.11
  20.9 0.1 pad_maximum_fusion.1.refs_0_
  20.9 3.3 %collective-permute-start.1 = (bf16[512,640]{1,0:T(8,128)(2,1)S(1)}, bf16[512,640]{1,0:T(8,128)(2,1)S(1)}, u32[]{:S(2)}, u32[]{:S(2)}) collective-permute-start(bf16[512,640]{1,0:T(8,128)(2,1)S(1)} %pad_maximum_fusion.1.refs_0_), channel_id=1, source_target_pairs={{0,32},{1,33},{2,34},{3,35},{4,36},{5,37},{6,38},{7,39},{8,40},{9,... | collective-permute-start | bytes 1966088 | tf_op jit(solution)/shard_map/ppermute | solution.py:41
  24.2 0.0 collective-permute-start.2
  24.2 0.0 collective-permute-done.5.refs_2_
  24.2 3.2 %collective-permute-start.6 = (bf16[512,640]{1,0:T(8,128)(2,1)S(1)}, bf16[512,640]{1,0:T(8,128)(2,1)S(1)}, u32[]{:S(2)}, u32[]{:S(2)}) collective-permute-start(bf16[512,640]{1,0:T(8,128)(2,1)S(1)} %constant_dynamic-update-slice_fusion.refs_3_), channel_id=1, source_target_pairs={{0,32},{1,33},{2,34},{3,35},{4,36},{5,37},{6,38},{7,39},{8,40},{9,... | collective-permute-start | bytes 1966088 | tf_op jit(solution)/shard_map/ppermute | solution.py:41
  27.5 11.9 %collective-permute-done.1.refs_1_ = bf16[512,640]{1,0:T(8,128)(2,1)S(1)} collective-permute-done((bf16[512,640]{1,0:T(8,128)(2,1)S(1)}, bf16[512,640]{1,0:T(8,128)(2,1)S(1)}, u32[]{:S(2)}, u32[]{:S(2)}) %collective-permute-start.1) | collective-permute-done | bytes 655392 | tf_op jit(solution)/shard_map/ppermute | solution.py:41
  39.4 0.0 collective-permute-start.10
  39.4 3.7 %collective-permute-done.2.refs_2_ = bf16[512,640]{1,0:T(8,128)(2,1)S(1)} collective-permute-done((bf16[512,640]{1,0:T(8,128)(2,1)S(1)}, bf16[512,640]{1,0:T(8,128)(2,1)S(1)}, u32[]{:S(2)}, u32[]{:S(2)}) %collective-permute-start.2) | collective-permute-done | bytes 655392 | tf_op jit(solution)/shard_map/ppermute | solution.py:41
  43.1 9.0 %collective-permute-done.6.refs_4_ = bf16[512,640]{1,0:T(8,128)(2,1)S(1)} collective-permute-done((bf16[512,640]{1,0:T(8,128)(2,1)S(1)}, bf16[512,640]{1,0:T(8,128)(2,1)S(1)}, u32[]{:S(2)}, u32[]{:S(2)}) %collective-permute-start.6) | collective-permute-done | bytes 655392 | tf_op jit(solution)/shard_map/ppermute | solution.py:41
  52.1 2.5 %collective-permute-done.7.refs_5_ = bf16[512,640]{1,0:T(8,128)(2,1)S(1)} collective-permute-done((bf16[512,640]{1,0:T(8,128)(2,1)S(1)}, bf16[512,640]{1,0:T(8,128)(2,1)S(1)}, u32[]{:S(2)}, u32[]{:S(2)}) %collective-permute-start.7) | collective-permute-done | bytes 655392 | tf_op jit(solution)/shard_map/ppermute | solution.py:41
  54.6 0.0 collective-permute-done.11.refs_8_
  54.6 0.0 collective-permute-start.12
  54.6 0.5 collective-permute-start.15
  55.1 0.3 collective-permute-start.13
  55.3 1.7 %collective-permute-start.14 = (bf16[512,640]{1,0:T(8,128)(2,1)S(1)}, bf16[512,640]{1,0:T(8,128)(2,1)S(1)}, u32[]{:S(2)}, u32[]{:S(2)}) collective-permute-start(bf16[512,640]{1,0:T(8,128)(2,1)S(1)} %collective-permute-done.7.refs_5_), channel_id=1, source_target_pairs={{0,96},{1,97},{2,98},{3,99},{4,100},{5,101},{6,102},{7,103},{8,104... | collective-permute-start | bytes 1966088 | tf_op jit(solution)/shard_map/ppermute | solution.py:41
  57.1 0.1 pad_add_fusion.core
  57.2 7.6 %collective-permute-done.15.refs_4_ = bf16[256,640]{1,0:T(8,128)(2,1)S(1)} collective-permute-done((bf16[256,640]{1,0:T(8,128)(2,1)S(1)}, bf16[256,640]{1,0:T(8,128)(2,1)S(1)}, u32[]{:S(2)}, u32[]{:S(2)}) %collective-permute-start.15) | collective-permute-done | bytes 327712 | tf_op jit(solution)/shard_map/ppermute | solution.py:41
  64.7 0.0 collective-permute-start.16
  64.7 0.5 collective-permute-start.17
  65.2 0.0 collective-permute-done.12.refs_9_
  65.3 6.0 %accumulate.1 = (f32[640,640]{1,0:T(8,128)S(1)}, f32[5,2,128,128]{3,2,1,0:T(8,128)S(1)}) custom-call(bf16[512,640]{1,0:T(8,128)(2,1)S(1)} %pad_maximum_fusion.1.refs_0_, bf16[512,640]{1,0:T(8,128)(2,1)S(1)} %collective-permute-done.1.refs_1_, bf16[512,640]{1,0:T(8,128)(2,1)S(1)} %collective-permute-done.2.refs_2_, ...), custom_call_target="tpu_custom_call" | custom-call | flops 3523215360 | bytes 11141120 | tf_op jit(solution)/shard_map/accumulate/pallas_call | solution.py:106
  71.3 0.6 collective-permute-done.13.refs_0_
  71.9 1.2 collective-permute-done.14.refs_1_
  73.1 5.1 %finish.1 = (bf16[2,4,208,128]{3,2,1,0:T(8,128)(2,1)S(1)}, bf16[2,4,208,128]{3,2,1,0:T(8,128)(2,1)S(1)}) custom-call(s32[2]{0:T(128)S(1)} %pad_add_fusion.core, f32[640,640]{1,0:T(8,128)S(1)} %get-tuple-element.18.s_prev, f32[5,2,128,128]{3,2,1,0:T(8,128)S(1)} %get-tuple-element.19.m_prev, bf16[512,640]{1,0:T(8,128)(2,1)S(1)} %collective-permute-done.13.refs_0_, ...), custom_call_target="tpu_custom_call" | custom-call | flops 2000000000 | bytes 5000000 | tf_op jit(solution)/shard_map/finish/pallas_call | solution.py:213
  78.3 0.1 collective-permute-start.18
  78.5 1.6 %collective-permute-done.18 = bf16[2,4,208,128]{3,2,1,0:T(8,128)(2,1)S(1)} collective-permute-done((bf16[2,4,208,128]{3,2,1,0:T(8,128)(2,1)S(1)}, bf16[2,4,208,128]{3,2,1,0:T(8,128)(2,1)S(1)}, u32[]{:S(2)}, u32[]{:S(2)}) %collective-permute-start.18) | collective-permute-done | bytes 426016 | tf_op jit(solution)/shard_map/ppermute | solution.py:41
  80.1 0.1 select_bitcast_fusion
  80.2 0.4 collective-permute-start.19
  80.6 1.7 %collective-permute-start.20 = (bf16[4,208,128]{2,1,0:T(8,128)(2,1)S(1)}, bf16[4,208,128]{2,1,0:T(8,128)(2,1)S(1)}, u32[]{:S(2)}, u32[]{:S(2)}) collective-permute-start(bf16[4,208,128]{2,1,0:T(8,128)(2,1)S(1)} %get-tuple-element.34), channel_id=1, source_target_pairs={{0,96},{1,97},{2,98},{3,99},{4,100},{5,101},{6,102},{7,103},{8,104... | collective-permute-start | bytes 638984 | tf_op jit(solution)/shard_map/ppermute | solution.py:41
  82.3 1.0 collective-permute-start.21
  83.3 0.1 broadcast_in_dim.3
  83.5 0.1 bitcast_dynamic-update-slice_fusion
  83.5 4.8 %collective-permute-done.19 = bf16[4,208,128]{2,1,0:T(8,128)(2,1)S(1)} collective-permute-done((bf16[4,208,128]{2,1,0:T(8,128)(2,1)S(1)}, bf16[4,208,128]{2,1,0:T(8,128)(2,1)S(1)}, u32[]{:S(2)}, u32[]{:S(2)}) %collective-permute-start.19) | collective-permute-done | bytes 213024 | tf_op jit(solution)/shard_map/ppermute | solution.py:41
  88.4 5.1 %collective-permute-done.20 = bf16[4,208,128]{2,1,0:T(8,128)(2,1)S(1)} collective-permute-done((bf16[4,208,128]{2,1,0:T(8,128)(2,1)S(1)}, bf16[4,208,128]{2,1,0:T(8,128)(2,1)S(1)}, u32[]{:S(2)}, u32[]{:S(2)}) %collective-permute-start.20) | collective-permute-done | bytes 213024 | tf_op jit(solution)/shard_map/ppermute | solution.py:41
  93.6 33.7 %all_to_all.5.src = bf16[16,208,128]{2,1,0:T(8,128)(2,1)S(1)} all-to-all(bf16[16,208,128]{2,1,0:T(8,128)(2,1)S(1)} %constant_dynamic-update-slice_fusion.4), channel_id=1, replica_groups=mesh['dp'=16,'owner'=16] {'owner'}, dimensions={0} | all-to-all | bytes 1703936 | tf_op jit(solution)/shard_map/all_to_all | solution.py:300
  127.3 1.2 unpack.1
  (15 shorter events, 0.2 us)
Async XLA Ops:
  0.0 4.8 %copy-start = (bf16[1,256,2560]{2,1,0:T(8,128)(2,1)S(1)}, bf16[1,256,2560]{2,1,0:T(8,128)(2,1)}, u32[]{:S(2)}) copy-start(bf16[1,256,2560]{2,1,0:T(8,128)(2,1)} %param.2) | copy-start | bytes 3932164
  1.5 10.7 %collective-permute-start.9 = (bf16[256,640]{1,0:T(8,128)(2,1)S(1)}, bf16[256,640]{1,0:T(8,128)(2,1)S(1)}, u32[]{:S(2)}, u32[]{:S(2)}) collective-permute-start(bf16[256,640]{1,0:T(8,128)(2,1)S(1)} %get-tuple-element.27), channel_id=1, source_target_pairs={{0,96},{1,97},{2,98},{3,99},{4,100},{5,101},{6,102},{7,103},{8,104... | collective-permute-start | bytes 983048 | tf_op jit(solution)/shard_map/ppermute | solution.py:41
  2.4 16.2 %collective-permute-start.8 = (bf16[256,640]{1,0:T(8,128)(2,1)S(1)}, bf16[256,640]{1,0:T(8,128)(2,1)S(1)}, u32[]{:S(2)}, u32[]{:S(2)}) collective-permute-start(bf16[256,640]{1,0:T(8,128)(2,1)S(1)} %get-tuple-element.28), channel_id=1, source_target_pairs={{0,32},{1,33},{2,34},{3,35},{4,36},{5,37},{6,38},{7,39},{8,40},{9,... | collective-permute-start | bytes 983048 | tf_op jit(solution)/shard_map/ppermute | solution.py:41
  4.9 13.7 %collective-permute-start.3 = (bf16[256,640]{1,0:T(8,128)(2,1)S(1)}, bf16[256,640]{1,0:T(8,128)(2,1)S(1)}, u32[]{:S(2)}, u32[]{:S(2)}) collective-permute-start(bf16[256,640]{1,0:T(8,128)(2,1)S(1)} %get-tuple-element.32), channel_id=1, source_target_pairs={{0,128},{1,129},{2,130},{3,131},{4,132},{5,133},{6,134},{7,135},{8... | collective-permute-start | bytes 983048 | tf_op jit(solution)/shard_map/ppermute | solution.py:41
  6.6 13.4 %collective-permute-start.4 = (bf16[256,640]{1,0:T(8,128)(2,1)S(1)}, bf16[256,640]{1,0:T(8,128)(2,1)S(1)}, u32[]{:S(2)}, u32[]{:S(2)}) collective-permute-start(bf16[256,640]{1,0:T(8,128)(2,1)S(1)} %get-tuple-element.29), channel_id=1, source_target_pairs={{0,144},{1,145},{2,146},{3,147},{4,148},{5,149},{6,150},{7,151},{8... | collective-permute-start | bytes 983048 | tf_op jit(solution)/shard_map/ppermute | solution.py:41
  6.6 14.3 %collective-permute-start = (bf16[256,640]{1,0:T(8,128)(2,1)S(1)}, bf16[256,640]{1,0:T(8,128)(2,1)S(1)}, u32[]{:S(2)}, u32[]{:S(2)}) collective-permute-start(bf16[256,640]{1,0:T(8,128)(2,1)S(1)} %get-tuple-element.30), channel_id=1, source_target_pairs={{0,16},{1,17},{2,18},{3,19},{4,20},{5,21},{6,22},{7,23},{8,24},{9,... | collective-permute-start | bytes 983048 | tf_op jit(solution)/shard_map/ppermute | solution.py:41
  12.2 12.0 %collective-permute-start.5 = (bf16[256,640]{1,0:T(8,128)(2,1)S(1)}, bf16[256,640]{1,0:T(8,128)(2,1)S(1)}, u32[]{:S(2)}, u32[]{:S(2)}) collective-permute-start(bf16[256,640]{1,0:T(8,128)(2,1)S(1)} %get-tuple-element.26), channel_id=1, source_target_pairs={{0,64},{1,65},{2,66},{3,67},{4,68},{5,69},{6,70},{7,71},{8,72},{9,... | collective-permute-start | bytes 983048 | tf_op jit(solution)/shard_map/ppermute | solution.py:41
  20.1 34.5 %collective-permute-start.11 = (bf16[768,640]{1,0:T(8,128)(2,1)S(1)}, bf16[768,640]{1,0:T(8,128)(2,1)S(1)}, u32[]{:S(2)}, u32[]{:S(2)}) collective-permute-start(bf16[768,640]{1,0:T(8,128)(2,1)S(1)} %pad_maximum_fusion.refs_6_), channel_id=1, source_target_pairs={{0,128},{1,129},{2,130},{3,131},{4,132},{5,133},{6,134},{7,135},{8... | collective-permute-start | bytes 2949128 | tf_op jit(solution)/shard_map/ppermute | solution.py:41
  20.9 18.5 %collective-permute-start.1 = (bf16[512,640]{1,0:T(8,128)(2,1)S(1)}, bf16[512,640]{1,0:T(8,128)(2,1)S(1)}, u32[]{:S(2)}, u32[]{:S(2)}) collective-permute-start(bf16[512,640]{1,0:T(8,128)(2,1)S(1)} %pad_maximum_fusion.1.refs_0_), channel_id=1, source_target_pairs={{0,32},{1,33},{2,34},{3,35},{4,36},{5,37},{6,38},{7,39},{8,40},{9,... | collective-permute-start | bytes 1966088 | tf_op jit(solution)/shard_map/ppermute | solution.py:41
  24.2 18.9 %collective-permute-start.2 = (bf16[512,640]{1,0:T(8,128)(2,1)S(1)}, bf16[512,640]{1,0:T(8,128)(2,1)S(1)}, u32[]{:S(2)}, u32[]{:S(2)}) collective-permute-start(bf16[512,640]{1,0:T(8,128)(2,1)S(1)} %pad_maximum_fusion.1.refs_0_), channel_id=1, source_target_pairs={{0,96},{1,97},{2,98},{3,99},{4,100},{5,101},{6,102},{7,103},{8,104... | collective-permute-start | bytes 1966088 | tf_op jit(solution)/shard_map/ppermute | solution.py:41
  24.2 27.9 %collective-permute-start.6 = (bf16[512,640]{1,0:T(8,128)(2,1)S(1)}, bf16[512,640]{1,0:T(8,128)(2,1)S(1)}, u32[]{:S(2)}, u32[]{:S(2)}) collective-permute-start(bf16[512,640]{1,0:T(8,128)(2,1)S(1)} %constant_dynamic-update-slice_fusion.refs_3_), channel_id=1, source_target_pairs={{0,32},{1,33},{2,34},{3,35},{4,36},{5,37},{6,38},{7,39},{8,40},{9,... | collective-permute-start | bytes 1966088 | tf_op jit(solution)/shard_map/ppermute | solution.py:41
  27.5 27.1 %collective-permute-start.7 = (bf16[512,640]{1,0:T(8,128)(2,1)S(1)}, bf16[512,640]{1,0:T(8,128)(2,1)S(1)}, u32[]{:S(2)}, u32[]{:S(2)}) collective-permute-start(bf16[512,640]{1,0:T(8,128)(2,1)S(1)} %constant_dynamic-update-slice_fusion.refs_3_), channel_id=1, source_target_pairs={{0,96},{1,97},{2,98},{3,99},{4,100},{5,101},{6,102},{7,103},{8,104... | collective-permute-start | bytes 1966088 | tf_op jit(solution)/shard_map/ppermute | solution.py:41
  39.4 25.3 %collective-permute-start.10 = (bf16[768,640]{1,0:T(8,128)(2,1)S(1)}, bf16[768,640]{1,0:T(8,128)(2,1)S(1)}, u32[]{:S(2)}, u32[]{:S(2)}) collective-permute-start(bf16[768,640]{1,0:T(8,128)(2,1)S(1)} %pad_maximum_fusion.refs_6_), channel_id=1, source_target_pairs={{0,16},{1,17},{2,18},{3,19},{4,20},{5,21},{6,22},{7,23},{8,24},{9,... | collective-permute-start | bytes 2949128 | tf_op jit(solution)/shard_map/ppermute | solution.py:41
  54.6 10.6 %collective-permute-start.12 = (bf16[768,640]{1,0:T(8,128)(2,1)S(1)}, bf16[768,640]{1,0:T(8,128)(2,1)S(1)}, u32[]{:S(2)}, u32[]{:S(2)}) collective-permute-start(bf16[768,640]{1,0:T(8,128)(2,1)S(1)} %collective-permute-done.11.refs_8_), channel_id=1, source_target_pairs={{0,16},{1,17},{2,18},{3,19},{4,20},{5,21},{6,22},{7,23},{8,24},{9,... | collective-permute-start | bytes 2949128 | tf_op jit(solution)/shard_map/ppermute | solution.py:41
  54.6 10.1 %collective-permute-start.15 = (bf16[256,640]{1,0:T(8,128)(2,1)S(1)}, bf16[256,640]{1,0:T(8,128)(2,1)S(1)}, u32[]{:S(2)}, u32[]{:S(2)}) collective-permute-start(bf16[256,640]{1,0:T(8,128)(2,1)S(1)} %collective-permute-done.5.refs_2_), channel_id=1, source_target_pairs={{0,128},{1,129},{2,130},{3,131},{4,132},{5,133},{6,134},{7,135},{8... | collective-permute-start | bytes 983048 | tf_op jit(solution)/shard_map/ppermute | solution.py:41
  55.1 16.9 %collective-permute-start.13 = (bf16[512,640]{1,0:T(8,128)(2,1)S(1)}, bf16[512,640]{1,0:T(8,128)(2,1)S(1)}, u32[]{:S(2)}, u32[]{:S(2)}) collective-permute-start(bf16[512,640]{1,0:T(8,128)(2,1)S(1)} %collective-permute-done.1.refs_1_), channel_id=1, source_target_pairs={{0,32},{1,33},{2,34},{3,35},{4,36},{5,37},{6,38},{7,39},{8,40},{9,... | collective-permute-start | bytes 1966088 | tf_op jit(solution)/shard_map/ppermute | solution.py:41
  55.3 17.8 %collective-permute-start.14 = (bf16[512,640]{1,0:T(8,128)(2,1)S(1)}, bf16[512,640]{1,0:T(8,128)(2,1)S(1)}, u32[]{:S(2)}, u32[]{:S(2)}) collective-permute-start(bf16[512,640]{1,0:T(8,128)(2,1)S(1)} %collective-permute-done.7.refs_5_), channel_id=1, source_target_pairs={{0,96},{1,97},{2,98},{3,99},{4,100},{5,101},{6,102},{7,103},{8,104... | collective-permute-start | bytes 1966088 | tf_op jit(solution)/shard_map/ppermute | solution.py:41
  64.7 8.4 %collective-permute-start.16 = (bf16[256,640]{1,0:T(8,128)(2,1)S(1)}, bf16[256,640]{1,0:T(8,128)(2,1)S(1)}, u32[]{:S(2)}, u32[]{:S(2)}) collective-permute-start(bf16[256,640]{1,0:T(8,128)(2,1)S(1)} %collective-permute-done.5.refs_2_), channel_id=1, source_target_pairs={{0,16},{1,17},{2,18},{3,19},{4,20},{5,21},{6,22},{7,23},{8,24},{9,... | collective-permute-start | bytes 983048 | tf_op jit(solution)/shard_map/ppermute | solution.py:41
  64.7 8.4 %collective-permute-start.17 = (bf16[256,640]{1,0:T(8,128)(2,1)S(1)}, bf16[256,640]{1,0:T(8,128)(2,1)S(1)}, u32[]{:S(2)}, u32[]{:S(2)}) collective-permute-start(bf16[256,640]{1,0:T(8,128)(2,1)S(1)} %collective-permute-done.15.refs_4_), channel_id=1, source_target_pairs={{0,16},{1,17},{2,18},{3,19},{4,20},{5,21},{6,22},{7,23},{8,24},{9,... | collective-permute-start | bytes 983048 | tf_op jit(solution)/shard_map/ppermute | solution.py:41
  78.3 1.9 %collective-permute-start.18 = (bf16[2,4,208,128]{3,2,1,0:T(8,128)(2,1)S(1)}, bf16[2,4,208,128]{3,2,1,0:T(8,128)(2,1)S(1)}, u32[]{:S(2)}, u32[]{:S(2)}) collective-permute-start(bf16[2,4,208,128]{3,2,1,0:T(8,128)(2,1)S(1)} %get-tuple-element.24), channel_id=1, source_target_pairs={{0,16},{1,17},{2,18},{3,19},{4,20},{5,21},{6,22},{7,23},{8,24},{9,... | collective-permute-start | bytes 1277960 | tf_op jit(solution)/shard_map/ppermute | solution.py:41
  80.2 8.2 %collective-permute-start.19 = (bf16[4,208,128]{2,1,0:T(8,128)(2,1)S(1)}, bf16[4,208,128]{2,1,0:T(8,128)(2,1)S(1)}, u32[]{:S(2)}, u32[]{:S(2)}) collective-permute-start(bf16[4,208,128]{2,1,0:T(8,128)(2,1)S(1)} %get-tuple-element.35), channel_id=1, source_target_pairs={{0,32},{1,33},{2,34},{3,35},{4,36},{5,37},{6,38},{7,39},{8,40},{9,... | collective-permute-start | bytes 638984 | tf_op jit(solution)/shard_map/ppermute | solution.py:41
  80.6 13.0 %collective-permute-start.20 = (bf16[4,208,128]{2,1,0:T(8,128)(2,1)S(1)}, bf16[4,208,128]{2,1,0:T(8,128)(2,1)S(1)}, u32[]{:S(2)}, u32[]{:S(2)}) collective-permute-start(bf16[4,208,128]{2,1,0:T(8,128)(2,1)S(1)} %get-tuple-element.34), channel_id=1, source_target_pairs={{0,96},{1,97},{2,98},{3,99},{4,100},{5,101},{6,102},{7,103},{8,104... | collective-permute-start | bytes 638984 | tf_op jit(solution)/shard_map/ppermute | solution.py:41
  82.3 11.3 %collective-permute-start.21 = (bf16[4,208,128]{2,1,0:T(8,128)(2,1)S(1)}, bf16[4,208,128]{2,1,0:T(8,128)(2,1)S(1)}, u32[]{:S(2)}, u32[]{:S(2)}) collective-permute-start(bf16[4,208,128]{2,1,0:T(8,128)(2,1)S(1)} %get-tuple-element.33), channel_id=1, source_target_pairs={{0,64},{1,65},{2,66},{3,67},{4,68},{5,69},{6,70},{7,71},{8,72},{9,... | collective-permute-start | bytes 638984 | tf_op jit(solution)/shard_map/ppermute | solution.py:41

commit v3 on v2

--- a/solution.py
+++ b/solution.py
@@ -149,7 +149,7 @@
 
 
 def finish_kernel(core, s_prev, m_prev, *refs):
-    keep, give, inv, upd = refs[6:]
+    give, inv, upd = refs[6:]
     tok = refs[2].shape[0]
     late = [(refs[n // 2], (n % 2) * tok, refs[2 + n]) for n in range(4)]
     rows = lax.broadcasted_iota(jnp.int32, (BLK, BLK), 0)
@@ -187,20 +187,27 @@
     for i in range(NB):
         blk = slice(i * BLK, (i + 1) * BLK)
         upd[blk, :] = dot_left(inv[2 * i].T, upd[blk, :])
-    for j in range(NB):
-        blk = slice(j * BLK, (j + 1) * BLK)
-        upd[:, blk] = dot_split(upd[:, blk], inv[2 * j + 1]) * (1.0 / math.sqrt(TOKENS))
-    for out, parity in ((keep, core[0]), (give, 1 - core[0])):
-        for b in range(2):
-            start = pl.multiple_of((2 * b + parity) * OUT, 32)
-            strip = upd[pl.ds(start, OUT), :]
-            for j in range(4):
-                piece = strip[:, j * OUT : (j + 1) * OUT]
-                tail = piece[:, BLK:]
-                packed = jnp.concatenate([tail[q * 40 : (q + 1) * 40] for q in range(4)], axis=1)
-                packed = jnp.concatenate([packed, jnp.zeros((8, BLK), F32)], axis=0)
-                out[b, j, :OUT, :] = piece[:, :BLK].astype(BF16)
-                out[b, j, OUT:, :] = packed.astype(BF16)
+    emit(give, 1 - core[0], upd, inv)
+
+
+def keep_kernel(core, upd, inv, keep):
+    emit(keep, core[0], upd, inv)
+
+
+def emit(out, parity, upd, inv):
+    for b in range(2):
+        start = pl.multiple_of((2 * b + parity) * OUT, 32)
+        left = upd[pl.ds(start, OUT), :]
+        strip = jnp.concatenate(
+            [dot_split(left[:, j * BLK : (j + 1) * BLK], inv[2 * j + 1]) for j in range(NB)], axis=1
+        ) * (1.0 / math.sqrt(TOKENS))
+        for j in range(4):
+            piece = strip[:, j * OUT : (j + 1) * OUT]
+            tail = piece[:, BLK:]
+            packed = jnp.concatenate([tail[q * 40 : (q + 1) * 40] for q in range(4)], axis=1)
+            packed = jnp.concatenate([packed, jnp.zeros((8, BLK), F32)], axis=0)
+            out[b, j, :OUT, :] = piece[:, :BLK].astype(BF16)
+            out[b, j, OUT:, :] = packed.astype(BF16)
 
 
 def finish(core, sums, a_late, g_arrays):
@@ -210,20 +217,34 @@
         return pl.BlockSpec(shape, lambda i, c: (0,) * len(shape))
 
     out = jax.ShapeDtypeStruct((2, 4, PACK, BLK), BF16)
+    inv = jax.ShapeDtypeStruct((2 * NB, BLK, BLK), F32)
+    left = jax.ShapeDtypeStruct((QUART, QUART), F32)
     return pl.pallas_call(
         finish_kernel,
         grid_spec=pltpu.PrefetchScalarGridSpec(
             num_scalar_prefetch=1,
             grid=(1,),
             in_specs=[whole(v.shape) for v in (*sums, *a_late)] + [whole((tok, QUART))] * 4,
-            out_specs=[whole(out.shape)] * 2,
-            scratch_shapes=[pltpu.VMEM((2 * NB, BLK, BLK), F32), pltpu.VMEM((QUART, QUART), F32)],
+            out_specs=[whole(out.shape), whole(inv.shape), whole(left.shape)],
         ),
-        out_shape=[out] * 2,
+        out_shape=[out, inv, left],
         compiler_params=params(),
         cost_estimate=pl.CostEstimate(flops=2 * 10**9, bytes_accessed=5 * 10**6, transcendentals=0),
         name="finish",
     )(core, *sums, *a_late, *g_arrays)
+
+
+def keep_strips(core, left, inv):
+    vmem = pl.BlockSpec(memory_space=pltpu.VMEM)
+    return pl.pallas_call(
+        keep_kernel,
+        in_specs=[pl.BlockSpec(memory_space=pltpu.SMEM), vmem, vmem],
+        out_specs=vmem,
+        out_shape=jax.ShapeDtypeStruct((2, 4, PACK, BLK), BF16),
+        compiler_params=params(),
+        cost_estimate=pl.CostEstimate(flops=10**9, bytes_accessed=5 * 10**6, transcendentals=0),
+        name="keep",
+    )(core, left, inv)
 
 
 def unpack_kernel(src, dst):
@@ -283,8 +304,9 @@
     g_late = []
     for block in lax.optimization_barrier((g_far, g_far_mate, mate_left, mate_right))[:2]:
         g_late += [block, send(block, swap_core)]
-    keep, give = finish(place, sums, [own_far, mate_far], g_late)
+    give, inv, left = finish(place, sums, [own_far, mate_far], g_late)
     recv = send(give, swap_core)
+    keep = keep_strips(place, left, inv)
     got = []
     for k, move in ((0, None), (1, plus_x), (3, minus_x), (2, far_x)):
         target = (x + k) % 4

time: 130 us -> 131 us (level)
  other arithmetic: 0.38 us -> 2.44 us
  waiting for transfers between devices: 60.7 us -> 58.9 us
    ppermute x22, waiting for transfers between devices: 60.7 us -> 58.9 us  [send(): return lax.ppermute(value, AXES, pairs(move))]
where the time goes in v3:
time: 131 us; the launch traced here: 129 us
  waiting for transfers between devices  58.9 us (45%)
  blocking collectives  33.7 us (26%)
  starting transfers between devices  19.3 us (15%)
  Pallas kernels  13 us (10%)
  other arithmetic  2.44 us (2%)
  local copies, waits for them, and re-layouts  1.88 us (1%)
    ppermute x22, waiting for transfers between devices, send(): return lax.ppermute(value, AXES, pairs(move))  58.9 us
    all_to_all x1, blocking collectives, local(): lax.all_to_all(pieces, 'owner', split_axis=0, concat_axis=0, tiled=True)  33.7 us
    ppermute x22, starting transfers between devices, send(): return lax.ppermute(value, AXES, pairs(move))  19.3 us
    pallas_call x1, Pallas kernels, accumulate(): pl.pallas_call(functools.partial(accumulate_kernel, plan, len(g_list), pr...  6.03 us
    pallas_call x1, Pallas kernels, finish(): pl.pallas_call(finish_kernel, grid_spec=pltpu.PrefetchScalarGridSpec(num_...  4.72 us
  transfers between devices with their start and end apart: 22, of which 13 were waited for; matrix products, arithmetic and copies ran while one was open for 1% of the time, Pallas kernels for 5%

profile of v3, /device:TPU:38, one launch (start us, length us, event | category | flops | bytes accessed | tf_op | source)
XLA Modules:
  0.0 129.4 jit_solution(1482944779921239483)
XLA Ops:
  0.0 1.5 %dynamic-slice_bitcast_fusion.2 = (bf16[256,640]{1,0:T(8,128)(2,1)S(1)}, bf16[256,640]{1,0:T(8,128)(2,1)S(1)}, bf16[256,640]{1,0:T(8,128)(2,1)S(1)}, bf16[256,640]{1,0:T(8,128)(2,1)S(1)}) fusion(bf16[1,256,2560]{2,1,0:T(8,128)(2,1)} %param.3, s32[]{:T(128)S(6)} %select_n.190, s32[]{:T(128)S(6)} %select_n.189, s32[]{:T(128)S(6)} %select_n.194, s32[]{:T(128)S(6)} %select_n.192), kind=kLoop, calls=%fused_computation.4 | loop fusion | bytes 2621456 | tf_op jit(solution)/shard_map/dynamic_slice | solution.py:69
  1.5 0.9 collective-permute-start.9
  2.4 2.4 %collective-permute-start.8 = (bf16[256,640]{1,0:T(8,128)(2,1)S(1)}, bf16[256,640]{1,0:T(8,128)(2,1)S(1)}, u32[]{:S(2)}, u32[]{:S(2)}) collective-permute-start(bf16[256,640]{1,0:T(8,128)(2,1)S(1)} %get-tuple-element.30), channel_id=1, source_target_pairs={{0,32},{1,33},{2,34},{3,35},{4,36},{5,37},{6,38},{7,39},{8,40},{9,... | collective-permute-start | bytes 983048 | tf_op jit(solution)/shard_map/ppermute | solution.py:41
  4.8 0.1 dynamic-slice_bitcast_fusion.4
  4.9 1.7 %collective-permute-start.3 = (bf16[256,640]{1,0:T(8,128)(2,1)S(1)}, bf16[256,640]{1,0:T(8,128)(2,1)S(1)}, u32[]{:S(2)}, u32[]{:S(2)}) collective-permute-start(bf16[256,640]{1,0:T(8,128)(2,1)S(1)} %get-tuple-element.34), channel_id=1, source_target_pairs={{0,128},{1,129},{2,130},{3,131},{4,132},{5,133},{6,134},{7,135},{8... | collective-permute-start | bytes 983048 | tf_op jit(solution)/shard_map/ppermute | solution.py:41
  6.6 0.0 collective-permute-start.4
  6.6 0.6 collective-permute-start
  7.2 5.1 %collective-permute-done.9 = bf16[256,640]{1,0:T(8,128)(2,1)S(1)} collective-permute-done((bf16[256,640]{1,0:T(8,128)(2,1)S(1)}, bf16[256,640]{1,0:T(8,128)(2,1)S(1)}, u32[]{:S(2)}, u32[]{:S(2)}) %collective-permute-start.9) | collective-permute-done | bytes 327712 | tf_op jit(solution)/shard_map/ppermute | solution.py:41
  12.2 0.2 collective-permute-start.5
  12.4 6.1 %collective-permute-done.8 = bf16[256,640]{1,0:T(8,128)(2,1)S(1)} collective-permute-done((bf16[256,640]{1,0:T(8,128)(2,1)S(1)}, bf16[256,640]{1,0:T(8,128)(2,1)S(1)}, u32[]{:S(2)}, u32[]{:S(2)}) %collective-permute-start.8) | collective-permute-done | bytes 327712 | tf_op jit(solution)/shard_map/ppermute | solution.py:41
  18.6 0.1 pad_maximum_fusion.refs_6_
  18.7 1.3 %collective-permute-done.4 = bf16[256,640]{1,0:T(8,128)(2,1)S(1)} collective-permute-done((bf16[256,640]{1,0:T(8,128)(2,1)S(1)}, bf16[256,640]{1,0:T(8,128)(2,1)S(1)}, u32[]{:S(2)}, u32[]{:S(2)}) %collective-permute-start.4) | collective-permute-done | bytes 327712 | tf_op jit(solution)/shard_map/ppermute | solution.py:41
  20.1 0.8 collective-permute-start.11
  20.9 0.0 collective-permute-done
  20.9 0.1 pad_maximum_fusion.1.refs_0_
  20.9 3.3 %collective-permute-start.1 = (bf16[512,640]{1,0:T(8,128)(2,1)S(1)}, bf16[512,640]{1,0:T(8,128)(2,1)S(1)}, u32[]{:S(2)}, u32[]{:S(2)}) collective-permute-start(bf16[512,640]{1,0:T(8,128)(2,1)S(1)} %pad_maximum_fusion.1.refs_0_), channel_id=1, source_target_pairs={{0,32},{1,33},{2,34},{3,35},{4,36},{5,37},{6,38},{7,39},{8,40},{9,... | collective-permute-start | bytes 1966088 | tf_op jit(solution)/shard_map/ppermute | solution.py:41
  24.2 3.2 %collective-permute-start.6 = (bf16[512,640]{1,0:T(8,128)(2,1)S(1)}, bf16[512,640]{1,0:T(8,128)(2,1)S(1)}, u32[]{:S(2)}, u32[]{:S(2)}) collective-permute-start(bf16[512,640]{1,0:T(8,128)(2,1)S(1)} %constant_dynamic-update-slice_fusion.refs_3_), channel_id=1, source_target_pairs={{0,32},{1,33},{2,34},{3,35},{4,36},{5,37},{6,38},{7,39},{8,40},{9,... | collective-permute-start | bytes 1966088 | tf_op jit(solution)/shard_map/ppermute | solution.py:41
  27.5 0.0 collective-permute-start.7
  27.5 11.9 %collective-permute-done.1.refs_1_ = bf16[512,640]{1,0:T(8,128)(2,1)S(1)} collective-permute-done((bf16[512,640]{1,0:T(8,128)(2,1)S(1)}, bf16[512,640]{1,0:T(8,128)(2,1)S(1)}, u32[]{:S(2)}, u32[]{:S(2)}) %collective-permute-start.1) | collective-permute-done | bytes 655392 | tf_op jit(solution)/shard_map/ppermute | solution.py:41
  39.4 0.0 collective-permute-start.10
  39.4 3.7 %collective-permute-done.2.refs_2_ = bf16[512,640]{1,0:T(8,128)(2,1)S(1)} collective-permute-done((bf16[512,640]{1,0:T(8,128)(2,1)S(1)}, bf16[512,640]{1,0:T(8,128)(2,1)S(1)}, u32[]{:S(2)}, u32[]{:S(2)}) %collective-permute-start.2) | collective-permute-done | bytes 655392 | tf_op jit(solution)/shard_map/ppermute | solution.py:41
  43.1 9.0 %collective-permute-done.6.refs_4_ = bf16[512,640]{1,0:T(8,128)(2,1)S(1)} collective-permute-done((bf16[512,640]{1,0:T(8,128)(2,1)S(1)}, bf16[512,640]{1,0:T(8,128)(2,1)S(1)}, u32[]{:S(2)}, u32[]{:S(2)}) %collective-permute-start.6) | collective-permute-done | bytes 655392 | tf_op jit(solution)/shard_map/ppermute | solution.py:41
  52.1 2.5 %collective-permute-done.7.refs_5_ = bf16[512,640]{1,0:T(8,128)(2,1)S(1)} collective-permute-done((bf16[512,640]{1,0:T(8,128)(2,1)S(1)}, bf16[512,640]{1,0:T(8,128)(2,1)S(1)}, u32[]{:S(2)}, u32[]{:S(2)}) %collective-permute-start.7) | collective-permute-done | bytes 655392 | tf_op jit(solution)/shard_map/ppermute | solution.py:41
  54.6 0.0 collective-permute-done.11.refs_8_
  54.6 0.5 collective-permute-start.15
  55.1 0.3 collective-permute-start.13
  55.3 1.7 %collective-permute-start.14 = (bf16[512,640]{1,0:T(8,128)(2,1)S(1)}, bf16[512,640]{1,0:T(8,128)(2,1)S(1)}, u32[]{:S(2)}, u32[]{:S(2)}) collective-permute-start(bf16[512,640]{1,0:T(8,128)(2,1)S(1)} %collective-permute-done.7.refs_5_), channel_id=1, source_target_pairs={{0,96},{1,97},{2,98},{3,99},{4,100},{5,101},{6,102},{7,103},{8,104... | collective-permute-start | bytes 1966088 | tf_op jit(solution)/shard_map/ppermute | solution.py:41
  57.1 0.1 pad_add_fusion.core
  57.2 7.6 %collective-permute-done.15.refs_4_ = bf16[256,640]{1,0:T(8,128)(2,1)S(1)} collective-permute-done((bf16[256,640]{1,0:T(8,128)(2,1)S(1)}, bf16[256,640]{1,0:T(8,128)(2,1)S(1)}, u32[]{:S(2)}, u32[]{:S(2)}) %collective-permute-start.15) | collective-permute-done | bytes 327712 | tf_op jit(solution)/shard_map/ppermute | solution.py:41
  64.7 0.5 collective-permute-start.17
  65.3 6.0 %accumulate.1 = (f32[640,640]{1,0:T(8,128)S(1)}, f32[5,2,128,128]{3,2,1,0:T(8,128)S(1)}) custom-call(bf16[512,640]{1,0:T(8,128)(2,1)S(1)} %pad_maximum_fusion.1.refs_0_, bf16[512,640]{1,0:T(8,128)(2,1)S(1)} %collective-permute-done.1.refs_1_, bf16[512,640]{1,0:T(8,128)(2,1)S(1)} %collective-permute-done.2.refs_2_, ...), custom_call_target="tpu_custom_call" | custom-call | flops 3523215360 | bytes 11141120 | tf_op jit(solution)/shard_map/accumulate/pallas_call | solution.py:106
  71.3 0.6 collective-permute-done.13.refs_0_
  71.9 1.2 collective-permute-done.14.refs_1_
  73.1 0.0 collective-permute-done.16.refs_3_
  73.1 4.7 %finish.1 = (bf16[2,4,208,128]{3,2,1,0:T(8,128)(2,1)S(1)}, f32[10,128,128]{2,1,0:T(8,128)S(1)}, f32[640,640]{1,0:T(8,128)S(1)}) custom-call(s32[2]{0:T(128)S(1)} %pad_add_fusion.core, f32[640,640]{1,0:T(8,128)S(1)} %get-tuple-element.19.s_prev, f32[5,2,128,128]{3,2,1,0:T(8,128)S(1)} %get-tuple-element.20.m_prev, ...), custom_call_target="tpu_custom_call" | custom-call | flops 2000000000 | bytes 5000000 | tf_op jit(solution)/shard_map/finish/pallas_call | solution.py:222
  77.9 0.1 collective-permute-start.18
  78.1 1.0 keep.1
  79.1 0.7 collective-permute-done.18
  79.9 1.2 select_bitcast_fusion
  81.1 0.4 collective-permute-start.19
  81.4 1.7 %collective-permute-start.20 = (bf16[4,208,128]{2,1,0:T(8,128)(2,1)S(1)}, bf16[4,208,128]{2,1,0:T(8,128)(2,1)S(1)}, u32[]{:S(2)}, u32[]{:S(2)}) collective-permute-start(bf16[4,208,128]{2,1,0:T(8,128)(2,1)S(1)} %get-tuple-element.36), channel_id=1, source_target_pairs={{0,96},{1,97},{2,98},{3,99},{4,100},{5,101},{6,102},{7,103},{8,104... | collective-permute-start | bytes 638984 | tf_op jit(solution)/shard_map/ppermute | solution.py:41
  83.2 1.0 collective-permute-start.21
  84.2 0.1 broadcast_in_dim.3
  84.3 1.0 bitcast_dynamic-update-slice_fusion
  85.3 3.9 %collective-permute-done.19 = bf16[4,208,128]{2,1,0:T(8,128)(2,1)S(1)} collective-permute-done((bf16[4,208,128]{2,1,0:T(8,128)(2,1)S(1)}, bf16[4,208,128]{2,1,0:T(8,128)(2,1)S(1)}, u32[]{:S(2)}, u32[]{:S(2)}) %collective-permute-start.19) | collective-permute-done | bytes 213024 | tf_op jit(solution)/shard_map/ppermute | solution.py:41
  89.3 5.1 %collective-permute-done.20 = bf16[4,208,128]{2,1,0:T(8,128)(2,1)S(1)} collective-permute-done((bf16[4,208,128]{2,1,0:T(8,128)(2,1)S(1)}, bf16[4,208,128]{2,1,0:T(8,128)(2,1)S(1)}, u32[]{:S(2)}, u32[]{:S(2)}) %collective-permute-start.20) | collective-permute-done | bytes 213024 | tf_op jit(solution)/shard_map/ppermute | solution.py:41
  94.5 33.7 %all_to_all.5.src = bf16[16,208,128]{2,1,0:T(8,128)(2,1)S(1)} all-to-all(bf16[16,208,128]{2,1,0:T(8,128)(2,1)S(1)} %constant_dynamic-update-slice_fusion.4), channel_id=1, replica_groups=mesh['dp'=16,'owner'=16] {'owner'}, dimensions={0} | all-to-all | bytes 1703936 | tf_op jit(solution)/shard_map/all_to_all | solution.py:322
  128.2 1.2 unpack.1
  (16 shorter events, 0.2 us)
Async XLA Ops:
  0.0 4.8 %copy-start = (bf16[1,256,2560]{2,1,0:T(8,128)(2,1)S(1)}, bf16[1,256,2560]{2,1,0:T(8,128)(2,1)}, u32[]{:S(2)}) copy-start(bf16[1,256,2560]{2,1,0:T(8,128)(2,1)} %param.2) | copy-start | bytes 3932164
  1.5 10.7 %collective-permute-start.9 = (bf16[256,640]{1,0:T(8,128)(2,1)S(1)}, bf16[256,640]{1,0:T(8,128)(2,1)S(1)}, u32[]{:S(2)}, u32[]{:S(2)}) collective-permute-start(bf16[256,640]{1,0:T(8,128)(2,1)S(1)} %get-tuple-element.29), channel_id=1, source_target_pairs={{0,96},{1,97},{2,98},{3,99},{4,100},{5,101},{6,102},{7,103},{8,104... | collective-permute-start | bytes 983048 | tf_op jit(solution)/shard_map/ppermute | solution.py:41
  2.4 16.2 %collective-permute-start.8 = (bf16[256,640]{1,0:T(8,128)(2,1)S(1)}, bf16[256,640]{1,0:T(8,128)(2,1)S(1)}, u32[]{:S(2)}, u32[]{:S(2)}) collective-permute-start(bf16[256,640]{1,0:T(8,128)(2,1)S(1)} %get-tuple-element.30), channel_id=1, source_target_pairs={{0,32},{1,33},{2,34},{3,35},{4,36},{5,37},{6,38},{7,39},{8,40},{9,... | collective-permute-start | bytes 983048 | tf_op jit(solution)/shard_map/ppermute | solution.py:41
  4.9 13.7 %collective-permute-start.3 = (bf16[256,640]{1,0:T(8,128)(2,1)S(1)}, bf16[256,640]{1,0:T(8,128)(2,1)S(1)}, u32[]{:S(2)}, u32[]{:S(2)}) collective-permute-start(bf16[256,640]{1,0:T(8,128)(2,1)S(1)} %get-tuple-element.34), channel_id=1, source_target_pairs={{0,128},{1,129},{2,130},{3,131},{4,132},{5,133},{6,134},{7,135},{8... | collective-permute-start | bytes 983048 | tf_op jit(solution)/shard_map/ppermute | solution.py:41
  6.6 13.4 %collective-permute-start.4 = (bf16[256,640]{1,0:T(8,128)(2,1)S(1)}, bf16[256,640]{1,0:T(8,128)(2,1)S(1)}, u32[]{:S(2)}, u32[]{:S(2)}) collective-permute-start(bf16[256,640]{1,0:T(8,128)(2,1)S(1)} %get-tuple-element.31), channel_id=1, source_target_pairs={{0,144},{1,145},{2,146},{3,147},{4,148},{5,149},{6,150},{7,151},{8... | collective-permute-start | bytes 983048 | tf_op jit(solution)/shard_map/ppermute | solution.py:41
  6.6 14.3 %collective-permute-start = (bf16[256,640]{1,0:T(8,128)(2,1)S(1)}, bf16[256,640]{1,0:T(8,128)(2,1)S(1)}, u32[]{:S(2)}, u32[]{:S(2)}) collective-permute-start(bf16[256,640]{1,0:T(8,128)(2,1)S(1)} %get-tuple-element.32), channel_id=1, source_target_pairs={{0,16},{1,17},{2,18},{3,19},{4,20},{5,21},{6,22},{7,23},{8,24},{9,... | collective-permute-start | bytes 983048 | tf_op jit(solution)/shard_map/ppermute | solution.py:41
  12.2 12.0 %collective-permute-start.5 = (bf16[256,640]{1,0:T(8,128)(2,1)S(1)}, bf16[256,640]{1,0:T(8,128)(2,1)S(1)}, u32[]{:S(2)}, u32[]{:S(2)}) collective-permute-start(bf16[256,640]{1,0:T(8,128)(2,1)S(1)} %get-tuple-element.28), channel_id=1, source_target_pairs={{0,64},{1,65},{2,66},{3,67},{4,68},{5,69},{6,70},{7,71},{8,72},{9,... | collective-permute-start | bytes 983048 | tf_op jit(solution)/shard_map/ppermute | solution.py:41
  20.1 34.5 %collective-permute-start.11 = (bf16[768,640]{1,0:T(8,128)(2,1)S(1)}, bf16[768,640]{1,0:T(8,128)(2,1)S(1)}, u32[]{:S(2)}, u32[]{:S(2)}) collective-permute-start(bf16[768,640]{1,0:T(8,128)(2,1)S(1)} %pad_maximum_fusion.refs_6_), channel_id=1, source_target_pairs={{0,128},{1,129},{2,130},{3,131},{4,132},{5,133},{6,134},{7,135},{8... | collective-permute-start | bytes 2949128 | tf_op jit(solution)/shard_map/ppermute | solution.py:41
  20.9 18.5 %collective-permute-start.1 = (bf16[512,640]{1,0:T(8,128)(2,1)S(1)}, bf16[512,640]{1,0:T(8,128)(2,1)S(1)}, u32[]{:S(2)}, u32[]{:S(2)}) collective-permute-start(bf16[512,640]{1,0:T(8,128)(2,1)S(1)} %pad_maximum_fusion.1.refs_0_), channel_id=1, source_target_pairs={{0,32},{1,33},{2,34},{3,35},{4,36},{5,37},{6,38},{7,39},{8,40},{9,... | collective-permute-start | bytes 1966088 | tf_op jit(solution)/shard_map/ppermute | solution.py:41
  24.2 18.9 %collective-permute-start.2 = (bf16[512,640]{1,0:T(8,128)(2,1)S(1)}, bf16[512,640]{1,0:T(8,128)(2,1)S(1)}, u32[]{:S(2)}, u32[]{:S(2)}) collective-permute-start(bf16[512,640]{1,0:T(8,128)(2,1)S(1)} %pad_maximum_fusion.1.refs_0_), channel_id=1, source_target_pairs={{0,96},{1,97},{2,98},{3,99},{4,100},{5,101},{6,102},{7,103},{8,104... | collective-permute-start | bytes 1966088 | tf_op jit(solution)/shard_map/ppermute | solution.py:41
  24.2 27.9 %collective-permute-start.6 = (bf16[512,640]{1,0:T(8,128)(2,1)S(1)}, bf16[512,640]{1,0:T(8,128)(2,1)S(1)}, u32[]{:S(2)}, u32[]{:S(2)}) collective-permute-start(bf16[512,640]{1,0:T(8,128)(2,1)S(1)} %constant_dynamic-update-slice_fusion.refs_3_), channel_id=1, source_target_pairs={{0,32},{1,33},{2,34},{3,35},{4,36},{5,37},{6,38},{7,39},{8,40},{9,... | collective-permute-start | bytes 1966088 | tf_op jit(solution)/shard_map/ppermute | solution.py:41
  27.5 27.1 %collective-permute-start.7 = (bf16[512,640]{1,0:T(8,128)(2,1)S(1)}, bf16[512,640]{1,0:T(8,128)(2,1)S(1)}, u32[]{:S(2)}, u32[]{:S(2)}) collective-permute-start(bf16[512,640]{1,0:T(8,128)(2,1)S(1)} %constant_dynamic-update-slice_fusion.refs_3_), channel_id=1, source_target_pairs={{0,96},{1,97},{2,98},{3,99},{4,100},{5,101},{6,102},{7,103},{8,104... | collective-permute-start | bytes 1966088 | tf_op jit(solution)/shard_map/ppermute | solution.py:41
  39.4 25.3 %collective-permute-start.10 = (bf16[768,640]{1,0:T(8,128)(2,1)S(1)}, bf16[768,640]{1,0:T(8,128)(2,1)S(1)}, u32[]{:S(2)}, u32[]{:S(2)}) collective-permute-start(bf16[768,640]{1,0:T(8,128)(2,1)S(1)} %pad_maximum_fusion.refs_6_), channel_id=1, source_target_pairs={{0,16},{1,17},{2,18},{3,19},{4,20},{5,21},{6,22},{7,23},{8,24},{9,... | collective-permute-start | bytes 2949128 | tf_op jit(solution)/shard_map/ppermute | solution.py:41
  54.6 10.6 %collective-permute-start.12 = (bf16[768,640]{1,0:T(8,128)(2,1)S(1)}, bf16[768,640]{1,0:T(8,128)(2,1)S(1)}, u32[]{:S(2)}, u32[]{:S(2)}) collective-permute-start(bf16[768,640]{1,0:T(8,128)(2,1)S(1)} %collective-permute-done.11.refs_8_), channel_id=1, source_target_pairs={{0,16},{1,17},{2,18},{3,19},{4,20},{5,21},{6,22},{7,23},{8,24},{9,... | collective-permute-start | bytes 2949128 | tf_op jit(solution)/shard_map/ppermute | solution.py:41
  54.6 10.1 %collective-permute-start.15 = (bf16[256,640]{1,0:T(8,128)(2,1)S(1)}, bf16[256,640]{1,0:T(8,128)(2,1)S(1)}, u32[]{:S(2)}, u32[]{:S(2)}) collective-permute-start(bf16[256,640]{1,0:T(8,128)(2,1)S(1)} %collective-permute-done.5.refs_2_), channel_id=1, source_target_pairs={{0,128},{1,129},{2,130},{3,131},{4,132},{5,133},{6,134},{7,135},{8... | collective-permute-start | bytes 983048 | tf_op jit(solution)/shard_map/ppermute | solution.py:41
  55.1 16.9 %collective-permute-start.13 = (bf16[512,640]{1,0:T(8,128)(2,1)S(1)}, bf16[512,640]{1,0:T(8,128)(2,1)S(1)}, u32[]{:S(2)}, u32[]{:S(2)}) collective-permute-start(bf16[512,640]{1,0:T(8,128)(2,1)S(1)} %collective-permute-done.1.refs_1_), channel_id=1, source_target_pairs={{0,32},{1,33},{2,34},{3,35},{4,36},{5,37},{6,38},{7,39},{8,40},{9,... | collective-permute-start | bytes 1966088 | tf_op jit(solution)/shard_map/ppermute | solution.py:41
  55.3 17.8 %collective-permute-start.14 = (bf16[512,640]{1,0:T(8,128)(2,1)S(1)}, bf16[512,640]{1,0:T(8,128)(2,1)S(1)}, u32[]{:S(2)}, u32[]{:S(2)}) collective-permute-start(bf16[512,640]{1,0:T(8,128)(2,1)S(1)} %collective-permute-done.7.refs_5_), channel_id=1, source_target_pairs={{0,96},{1,97},{2,98},{3,99},{4,100},{5,101},{6,102},{7,103},{8,104... | collective-permute-start | bytes 1966088 | tf_op jit(solution)/shard_map/ppermute | solution.py:41
  64.7 8.4 %collective-permute-start.16 = (bf16[256,640]{1,0:T(8,128)(2,1)S(1)}, bf16[256,640]{1,0:T(8,128)(2,1)S(1)}, u32[]{:S(2)}, u32[]{:S(2)}) collective-permute-start(bf16[256,640]{1,0:T(8,128)(2,1)S(1)} %collective-permute-done.5.refs_2_), channel_id=1, source_target_pairs={{0,16},{1,17},{2,18},{3,19},{4,20},{5,21},{6,22},{7,23},{8,24},{9,... | collective-permute-start | bytes 983048 | tf_op jit(solution)/shard_map/ppermute | solution.py:41
  64.7 8.4 %collective-permute-start.17 = (bf16[256,640]{1,0:T(8,128)(2,1)S(1)}, bf16[256,640]{1,0:T(8,128)(2,1)S(1)}, u32[]{:S(2)}, u32[]{:S(2)}) collective-permute-start(bf16[256,640]{1,0:T(8,128)(2,1)S(1)} %collective-permute-done.15.refs_4_), channel_id=1, source_target_pairs={{0,16},{1,17},{2,18},{3,19},{4,20},{5,21},{6,22},{7,23},{8,24},{9,... | collective-permute-start | bytes 983048 | tf_op jit(solution)/shard_map/ppermute | solution.py:41
  77.9 2.0 %collective-permute-start.18 = (bf16[2,4,208,128]{3,2,1,0:T(8,128)(2,1)S(1)}, bf16[2,4,208,128]{3,2,1,0:T(8,128)(2,1)}, u32[]{:S(2)}, u32[]{:S(2)}) collective-permute-start(bf16[2,4,208,128]{3,2,1,0:T(8,128)(2,1)S(1)} %get-tuple-element.26), channel_id=1, source_target_pairs={{0,16},{1,17},{2,18},{3,19},{4,20},{5,21},{6,22},{7,23},{8,24},{9,... | collective-permute-start | bytes 1277960 | tf_op jit(solution)/shard_map/ppermute | solution.py:41
  81.1 8.2 %collective-permute-start.19 = (bf16[4,208,128]{2,1,0:T(8,128)(2,1)S(1)}, bf16[4,208,128]{2,1,0:T(8,128)(2,1)S(1)}, u32[]{:S(2)}, u32[]{:S(2)}) collective-permute-start(bf16[4,208,128]{2,1,0:T(8,128)(2,1)S(1)} %get-tuple-element.37), channel_id=1, source_target_pairs={{0,32},{1,33},{2,34},{3,35},{4,36},{5,37},{6,38},{7,39},{8,40},{9,... | collective-permute-start | bytes 638984 | tf_op jit(solution)/shard_map/ppermute | solution.py:41
  81.4 13.0 %collective-permute-start.20 = (bf16[4,208,128]{2,1,0:T(8,128)(2,1)S(1)}, bf16[4,208,128]{2,1,0:T(8,128)(2,1)S(1)}, u32[]{:S(2)}, u32[]{:S(2)}) collective-permute-start(bf16[4,208,128]{2,1,0:T(8,128)(2,1)S(1)} %get-tuple-element.36), channel_id=1, source_target_pairs={{0,96},{1,97},{2,98},{3,99},{4,100},{5,101},{6,102},{7,103},{8,104... | collective-permute-start | bytes 638984 | tf_op jit(solution)/shard_map/ppermute | solution.py:41
  83.2 11.3 %collective-permute-start.21 = (bf16[4,208,128]{2,1,0:T(8,128)(2,1)S(1)}, bf16[4,208,128]{2,1,0:T(8,128)(2,1)S(1)}, u32[]{:S(2)}, u32[]{:S(2)}) collective-permute-start(bf16[4,208,128]{2,1,0:T(8,128)(2,1)S(1)} %get-tuple-element.35), channel_id=1, source_target_pairs={{0,64},{1,65},{2,66},{3,67},{4,68},{5,69},{6,70},{7,71},{8,72},{9,... | collective-permute-start | bytes 638984 | tf_op jit(solution)/shard_map/ppermute | solution.py:41
